TPU v7x, 32 devices: a whole 2x2x4 slice. The times are simulated.
32 devices in a mesh: dp: 4 (over z), row: 2 (over y), col: 4 (over x, core).
Axes of the slice: x: 2, y: 2, z: 4, core: 2. Of those that a mesh axis runs over, the one named last changes fastest.
Arguments:
- hidden_in: bfloat16 [32768, 960], P(('dp', 'row', 'col')), may hold values from -30 to 30
- cotangent: bfloat16 [32768, 960], P(('dp', 'row', 'col')), may hold values from -6 to 6
- segment_ids: int32 [32768], P(('dp', 'row', 'col')), may hold values from 0 to 6, as said below
- positions: int32 [32768], P(('dp', 'row', 'col')), may hold values from 0 to 2047, as said below
- query_weight: float32 [960, 960], P('row', 'col'), may hold values from -0.1875 to 0.1875
- key_weight: float32 [960, 320], P('row', 'col'), may hold values from -0.1875 to 0.1875
- value_weight: float32 [960, 320], P('row', 'col'), may hold values from -0.1875 to 0.1875
- output_weight: float32 [960, 960], P('row', 'col'), may hold values from -0.75 to 0.75
- gate_up_weight: float32 [2, 960, 2560], P(None, 'row', 'col'), may hold values from -0.1875 to 0.1875
- down_weight: float32 [960, 2560], P('row', 'col'), may hold values from -0.125 to 0.125
- norm_gains: float32 [2, 960], replicated, may hold values from 0.5 to 1.5
- query_moment: float32 [960, 960], P('row', 'col'), may hold values from -256 to 256
- key_moment: float32 [960, 320], P('row', 'col'), may hold values from -256 to 256
- value_moment: float32 [960, 320], P('row', 'col'), may hold values from -256 to 256
- output_moment: float32 [960, 960], P('row', 'col'), may hold values from -64 to 64
- gate_up_moment: float32 [2, 960, 2560], P(None, 'row', 'col'), may hold values from -64 to 64
- down_moment: float32 [960, 2560], P('row', 'col'), may hold values from -128 to 128
- gains_moment: float32 [2, 960], replicated, may hold values from -128 to 128
- query_square: float32 [960, 960], P('row', 'col'), may hold values from 6553.6 to 26214.4
- key_square: float32 [960, 320], P('row', 'col'), may hold values from 6553.6 to 26214.4
- value_square: float32 [960, 320], P('row', 'col'), may hold values from 6553.6 to 26214.4
- output_square: float32 [960, 960], P('row', 'col'), may hold values from 409.6 to 1638.4
- gate_up_square: float32 [2, 960, 2560], P(None, 'row', 'col'), may hold values from 409.6 to 1638.4
- down_square: float32 [960, 2560], P('row', 'col'), may hold values from 1638.4 to 6553.6
- gains_square: float32 [2, 960], replicated, may hold values from 1638.4 to 6553.6
Outputs:
- block_out: bfloat16 [32768, 960], P(('dp', 'row', 'col'))
- input_grad: bfloat16 [32768, 960], P(('dp', 'row', 'col'))
- query_grad: float32 [960, 960], P('row', 'col')
- query_moment_new: float32 [960, 960], P('row', 'col')
- query_square_new: float32 [960, 960], P('row', 'col')
- query_new: float32 [960, 960], P('row', 'col')
- key_grad: float32 [960, 320], P('row', 'col')
- key_moment_new: float32 [960, 320], P('row', 'col')
- key_square_new: float32 [960, 320], P('row', 'col')
- key_new: float32 [960, 320], P('row', 'col')
- value_grad: float32 [960, 320], P('row', 'col')
- value_moment_new: float32 [960, 320], P('row', 'col')
- value_square_new: float32 [960, 320], P('row', 'col')
- value_new: float32 [960, 320], P('row', 'col')
- output_grad: float32 [960, 960], P('row', 'col')
- output_moment_new: float32 [960, 960], P('row', 'col')
- output_square_new: float32 [960, 960], P('row', 'col')
- output_new: float32 [960, 960], P('row', 'col')
- gate_up_grad: float32 [2, 960, 2560], P(None, 'row', 'col')
- gate_up_moment_new: float32 [2, 960, 2560], P(None, 'row', 'col')
- gate_up_square_new: float32 [2, 960, 2560], P(None, 'row', 'col')
- gate_up_new: float32 [2, 960, 2560], P(None, 'row', 'col')
- down_grad: float32 [960, 2560], P('row', 'col')
- down_moment_new: float32 [960, 2560], P('row', 'col')
- down_square_new: float32 [960, 2560], P('row', 'col')
- down_new: float32 [960, 2560], P('row', 'col')
- gains_grad: float32 [2, 960], replicated
- gains_moment_new: float32 [2, 960], replicated
- gains_square_new: float32 [2, 960], replicated
- gains_new: float32 [2, 960], replicated
Inputs may be any that keep to these rules, and one draw needn't show every extreme that they name: `segment_ids`: within each sequence (a run of 1024 consecutive tokens) the segment number starts at 0 and never falls; tokens with one number form one document. `positions`: A token's position rises by one along its segment; a segment that begins inside a sequence begins at 0, while a sequence's first segment may continue a document that began before it.
All inputs are finite; a program needn't handle non-finite values.
Results may differ from a plain program's by a relative error of at most 0.017.
Values may be sent and summed in bfloat16 or wider, within the bound.
A program may use at most 256 MiB of HBM per device.

v0:
```python
import math

import jax
import jax.numpy as jnp
from jax import lax
from jax.sharding import PartitionSpec as P

HEADS = 15
KV_HEADS = 5
HEAD_DIM = 64
SEQ = 1024
STEP = 10


norm_eps = 1e-05
rope_base = 100000.0
beta_one = 0.9
beta_two = 0.95
adam_eps = 1e-08
decay_rate = 0.1
matrix_rate = 0.1
gain_rate = 1.0
masked_fill = -1000000000.0


def rope_tables(positions):
    ladder = jnp.arange(HEAD_DIM // 2, dtype=jnp.float32) * (2.0 / HEAD_DIM)
    frequency = jnp.exp(ladder * -math.log(rope_base))
    angles = positions.astype(jnp.float32)[:, None] * frequency[None, :]
    return (jnp.cos(angles), jnp.sin(angles))


def rotate(values, cos_table, sine_table):
    half_dim = HEAD_DIM // 2
    first_half = values[..., :half_dim]
    second_half = values[..., half_dim:]
    cos_rows = cos_table[:, None, :]
    sin_rows = sine_table[:, None, :]
    return jnp.concatenate(
        [
            first_half * cos_rows - second_half * sin_rows,
            second_half * cos_rows + first_half * sin_rows,
        ],
        axis=-1,
    )


def unrotate(incoming, cos_table, sine_table):
    half_dim = HEAD_DIM // 2
    first_half = incoming[..., :half_dim]
    second_half = incoming[..., half_dim:]
    cos_rows = cos_table[:, None, :]
    sin_rows = sine_table[:, None, :]
    return jnp.concatenate(
        [
            first_half * cos_rows + second_half * sin_rows,
            second_half * cos_rows - first_half * sin_rows,
        ],
        axis=-1,
    )


def allowed_pairs(segments):
    places = jnp.arange(segments.shape[0])
    return (places[:, None] >= places[None, :]) & (segments[:, None] == segments[None, :])


def scaled_scores(queries, key_rows, segments):
    scores = jnp.einsum(
        "gqd,sd->gqs", queries, key_rows, preferred_element_type=jnp.float32
    ) * HEAD_DIM ** (-0.5)
    return jnp.where(allowed_pairs(segments)[None], scores, masked_fill)


def head_forward(packed):
    queries, key_rows, value_rows, segments = packed
    scores = scaled_scores(queries, key_rows, segments)
    summit = jnp.max(scores, axis=-1, keepdims=True)
    powers = jnp.exp(scores - summit)
    totals = jnp.sum(powers, axis=-1, keepdims=True)
    softmaxed = (powers / totals).astype(jnp.bfloat16)
    blended = jnp.einsum("gqs,sd->gqd", softmaxed, value_rows, preferred_element_type=jnp.float32)
    return (blended.astype(jnp.bfloat16), (summit + jnp.log(totals))[..., 0])


def head_backward(packed):
    queries, key_rows, value_rows, out_grad, log_totals, segments = packed
    scores = scaled_scores(queries, key_rows, segments)
    chances = jnp.exp(scores - log_totals[..., None])
    value_grad = jnp.einsum(
        "gqs,gqd->sd", chances.astype(jnp.bfloat16), out_grad, preferred_element_type=jnp.float32
    )
    chance_grad = jnp.einsum(
        "gqd,sd->gqs", out_grad, value_rows, preferred_element_type=jnp.float32
    )
    centre = jnp.sum(chances * chance_grad, axis=-1, keepdims=True)
    score_grad = (chances * (chance_grad - centre)).astype(jnp.bfloat16)
    query_grad = jnp.einsum(
        "gqs,sd->gqd", score_grad, key_rows, preferred_element_type=jnp.float32
    ) * HEAD_DIM ** (-0.5)
    key_grad = jnp.einsum(
        "gqs,gqd->sd", score_grad, queries, preferred_element_type=jnp.float32
    ) * HEAD_DIM ** (-0.5)
    return (query_grad, key_grad, value_grad)


def query_heads(flat_rows):
    seq_count = flat_rows.shape[0] // SEQ
    group_size = HEADS // KV_HEADS
    shaped = flat_rows.reshape(seq_count, SEQ, KV_HEADS, group_size, HEAD_DIM).transpose(
        0, 2, 3, 1, 4
    )
    return shaped.reshape(seq_count * KV_HEADS, group_size, SEQ, HEAD_DIM)


def query_flat(head_rows):
    seq_count = head_rows.shape[0] // KV_HEADS
    group_size = head_rows.shape[1]
    shaped = head_rows.reshape(seq_count, KV_HEADS, group_size, SEQ, HEAD_DIM).transpose(
        0, 3, 1, 2, 4
    )
    return shaped.reshape(seq_count * SEQ, KV_HEADS * group_size * HEAD_DIM)


def shared_heads(flat_rows):
    seq_count = flat_rows.shape[0] // SEQ
    shaped = flat_rows.reshape(seq_count, SEQ, KV_HEADS, HEAD_DIM).transpose(0, 2, 1, 3)
    return shaped.reshape(seq_count * KV_HEADS, SEQ, HEAD_DIM)


def shared_flat(head_rows):
    seq_count = head_rows.shape[0] // KV_HEADS
    shaped = head_rows.reshape(seq_count, KV_HEADS, SEQ, HEAD_DIM).transpose(0, 2, 1, 3)
    return shaped.reshape(seq_count * SEQ, KV_HEADS * HEAD_DIM)


def to_grid(stack, row_count, col_count):
    return stack.reshape((row_count, col_count) + stack.shape[1:])


def project(inputs, grid):
    count_rows = inputs.shape[0]
    shaped = inputs.reshape(count_rows, grid.shape[0], grid.shape[2])
    result = jnp.einsum("tra,rcab->tcb", shaped, grid, preferred_element_type=jnp.float32)
    return result.reshape(count_rows, grid.shape[1] * grid.shape[3])


def project_back(incoming, grid):
    count_rows = incoming.shape[0]
    shaped = incoming.reshape(count_rows, grid.shape[1], grid.shape[3])
    result = jnp.einsum("tcb,rcab->tra", shaped, grid, preferred_element_type=jnp.float32)
    return result.reshape(count_rows, grid.shape[0] * grid.shape[2])


def grid_grad(inputs, incoming, grid):
    count_rows = inputs.shape[0]
    left_side = inputs.reshape(count_rows, grid.shape[0], grid.shape[2])
    right_side = incoming.reshape(count_rows, grid.shape[1], grid.shape[3])
    result = jnp.einsum("tra,tcb->rcab", left_side, right_side, preferred_element_type=jnp.float32)
    return result.reshape((grid.shape[0] * grid.shape[1],) + grid.shape[2:])


def norm_backward(inputs, inverse, scales, incoming):
    weighted = incoming * scales
    gain_part = jnp.sum(incoming * inputs * inverse, axis=0)
    input_part = inverse * weighted - inputs * inverse**3 * jnp.mean(
        weighted * inputs, axis=-1, keepdims=True
    )
    return (gain_part, input_part)


def adam_step(weight, gradient, moment, square, step_rate, decay_factor):
    moment_new = beta_one * moment + (1.0 - beta_one) * gradient
    square_new = beta_two * square + (1.0 - beta_two) * gradient * gradient
    scaled_step = (
        moment_new
        / (1.0 - beta_one**STEP)
        / (jnp.sqrt(square_new / (1.0 - beta_two**STEP)) + adam_eps)
    )
    return (moment_new, square_new, weight - step_rate * (scaled_step + decay_factor * weight))


def shards(
    hidden_in,
    cotangent,
    segment_ids,
    positions,
    query_weight,
    key_weight,
    value_weight,
    output_weight,
    gate_up_weight,
    down_weight,
    norm_gains,
    query_moment,
    key_moment,
    value_moment,
    output_moment,
    gate_up_moment,
    down_moment,
    gains_moment,
    query_square,
    key_square,
    value_square,
    output_square,
    gate_up_square,
    down_square,
    gains_square,
):
    row_count = lax.axis_size("row")
    col_count = lax.axis_size("col")
    token_count = hidden_in.shape[0]
    query_low = query_weight.astype(jnp.bfloat16)
    key_low = key_weight.astype(jnp.bfloat16)
    value_low = value_weight.astype(jnp.bfloat16)
    output_low = output_weight.astype(jnp.bfloat16)
    gate_up_low = gate_up_weight.astype(jnp.bfloat16)
    down_low = down_weight.astype(jnp.bfloat16)
    stacked = (
        lax.all_gather(query_low[None], ("row", "col"), axis=0, tiled=True),
        lax.all_gather(key_low[None], ("row", "col"), axis=0, tiled=True),
        lax.all_gather(value_low[None], ("row", "col"), axis=0, tiled=True),
        lax.all_gather(output_low[None], ("row", "col"), axis=0, tiled=True),
        lax.all_gather(gate_up_low[None], ("row", "col"), axis=0, tiled=True),
        lax.all_gather(down_low[None], ("row", "col"), axis=0, tiled=True),
    )
    gate_up_grid = to_grid(stacked[4], row_count, col_count)
    down_grid = to_grid(stacked[5], row_count, col_count)
    query_grid = to_grid(stacked[0], row_count, col_count)
    key_grid = to_grid(stacked[1], row_count, col_count)
    value_grid = to_grid(stacked[2], row_count, col_count)
    output_grid = to_grid(stacked[3], row_count, col_count)
    inputs = hidden_in.astype(jnp.float32)
    inverse_one = lax.rsqrt(jnp.mean(inputs * inputs, axis=-1, keepdims=True) + norm_eps)
    normed_one = (inputs * inverse_one * norm_gains[0]).astype(jnp.bfloat16)
    query_pre = project(normed_one, query_grid)
    key_pre = project(normed_one, key_grid)
    value_rows = project(normed_one, value_grid).astype(jnp.bfloat16)
    cos_table, sine_table = rope_tables(positions)
    queries = (
        rotate(query_pre.reshape(token_count, HEADS, HEAD_DIM), cos_table, sine_table)
        .astype(jnp.bfloat16)
        .reshape(token_count, HEADS * HEAD_DIM)
    )
    key_rows = (
        rotate(key_pre.reshape(token_count, KV_HEADS, HEAD_DIM), cos_table, sine_table)
        .astype(jnp.bfloat16)
        .reshape(token_count, KV_HEADS * HEAD_DIM)
    )
    head_segments = jnp.repeat(segment_ids.reshape(token_count // SEQ, SEQ), KV_HEADS, axis=0)
    query_split = query_heads(queries)
    key_split = shared_heads(key_rows)
    value_split = shared_heads(value_rows)
    blended_heads, log_totals = lax.map(
        head_forward, (query_split, key_split, value_split, head_segments)
    )
    blended = query_flat(blended_heads)
    middle = inputs + project(blended, output_grid)
    inverse_two = lax.rsqrt(jnp.mean(middle * middle, axis=-1, keepdims=True) + norm_eps)
    normed_two = (middle * inverse_two * norm_gains[1]).astype(jnp.bfloat16)
    normed_split = normed_two.reshape(token_count, row_count, -1)
    paired = jnp.einsum(
        "tra,rcgab->gtcb", normed_split, gate_up_grid, preferred_element_type=jnp.float32
    ).reshape(2, token_count, -1)
    gate_pre = paired[0]
    up_pre = paired[1]
    sigmoid_gate = 1.0 / (1.0 + jnp.exp(-gate_pre))
    silu_gate = gate_pre / (1.0 + jnp.exp(-gate_pre))
    hidden = (silu_gate * up_pre).astype(jnp.bfloat16)
    hidden_split = hidden.reshape(token_count, col_count, -1)
    mlp_out = jnp.einsum(
        "tcf,rcaf->tra", hidden_split, down_grid, preferred_element_type=jnp.float32
    ).reshape(token_count, -1)
    back_split = cotangent.reshape(token_count, row_count, -1)
    hidden_grad = jnp.einsum(
        "tra,rcaf->tcf", back_split, down_grid, preferred_element_type=jnp.float32
    ).reshape(token_count, -1)
    gate_grad = (
        hidden_grad * up_pre * sigmoid_gate * (1.0 + gate_pre * (1.0 - sigmoid_gate))
    ).astype(jnp.bfloat16)
    up_grad = (hidden_grad * silu_gate).astype(jnp.bfloat16)
    pair_grad = jnp.stack([gate_grad, up_grad]).reshape(2, token_count, col_count, -1)
    down_block = jnp.einsum(
        "tra,tcf->rcaf", back_split, hidden_split, preferred_element_type=jnp.float32
    ).reshape((row_count * col_count,) + down_grid.shape[2:])
    gate_up_block = jnp.einsum(
        "tra,gtcb->rcgab", normed_split, pair_grad, preferred_element_type=jnp.float32
    ).reshape((row_count * col_count,) + gate_up_grid.shape[2:])
    normed_two_grad = jnp.einsum(
        "gtcb,rcgab->tra", pair_grad, gate_up_grid, preferred_element_type=jnp.float32
    ).reshape(token_count, -1)
    block_out = (middle + mlp_out).astype(jnp.bfloat16)
    gain_two, middle_part = norm_backward(middle, inverse_two, norm_gains[1], normed_two_grad)
    middle_grad = cotangent.astype(jnp.float32) + middle_part
    middle_low = middle_grad.astype(jnp.bfloat16)
    output_block = grid_grad(blended, middle_low, output_grid)
    blended_grad = project_back(middle_low, output_grid).astype(jnp.bfloat16)
    query_back, key_back, value_back = lax.map(
        head_backward,
        (query_split, key_split, value_split, query_heads(blended_grad), log_totals, head_segments),
    )
    query_rot_grad = query_flat(query_back).reshape(token_count, HEADS, HEAD_DIM)
    key_rot_grad = shared_flat(key_back).reshape(token_count, KV_HEADS, HEAD_DIM)
    query_pre_grad = (
        unrotate(query_rot_grad, cos_table, sine_table)
        .reshape(token_count, HEADS * HEAD_DIM)
        .astype(jnp.bfloat16)
    )
    key_pre_grad = (
        unrotate(key_rot_grad, cos_table, sine_table)
        .reshape(token_count, KV_HEADS * HEAD_DIM)
        .astype(jnp.bfloat16)
    )
    value_pre_grad = shared_flat(value_back).astype(jnp.bfloat16)
    query_block = grid_grad(normed_one, query_pre_grad, query_grid)
    key_block = grid_grad(normed_one, key_pre_grad, key_grid)
    value_block = grid_grad(normed_one, value_pre_grad, value_grid)
    normed_one_grad = (
        project_back(query_pre_grad, query_grid)
        + project_back(key_pre_grad, key_grid)
        + project_back(value_pre_grad, value_grid)
    )
    gain_one, input_part = norm_backward(inputs, inverse_one, norm_gains[0], normed_one_grad)
    input_grad = (middle_grad + input_part).astype(jnp.bfloat16)
    summed = (
        lax.psum_scatter(query_block, ("row", "col"), scatter_dimension=0, tiled=True),
        lax.psum_scatter(key_block, ("row", "col"), scatter_dimension=0, tiled=True),
        lax.psum_scatter(value_block, ("row", "col"), scatter_dimension=0, tiled=True),
        lax.psum_scatter(output_block, ("row", "col"), scatter_dimension=0, tiled=True),
        lax.psum_scatter(gate_up_block, ("row", "col"), scatter_dimension=0, tiled=True),
        lax.psum_scatter(down_block, ("row", "col"), scatter_dimension=0, tiled=True),
    )
    query_sum = summed[0][0]
    key_sum = summed[1][0]
    value_sum = summed[2][0]
    output_sum = summed[3][0]
    gate_up_sum = summed[4][0]
    down_sum = summed[5][0]
    reduced = (
        lax.psum(query_sum.astype(jnp.bfloat16), "dp").astype(jnp.float32),
        lax.psum(key_sum.astype(jnp.bfloat16), "dp").astype(jnp.float32),
        lax.psum(value_sum.astype(jnp.bfloat16), "dp").astype(jnp.float32),
        lax.psum(output_sum.astype(jnp.bfloat16), "dp").astype(jnp.float32),
        lax.psum(gate_up_sum.astype(jnp.bfloat16), "dp").astype(jnp.float32),
        lax.psum(down_sum.astype(jnp.bfloat16), "dp").astype(jnp.float32),
    )
    gains_grad = lax.psum(jnp.stack([gain_one, gain_two]), ("dp", "row", "col"))
    query_update = adam_step(
        query_weight, reduced[0], query_moment, query_square, matrix_rate, decay_rate
    )
    key_update = adam_step(key_weight, reduced[1], key_moment, key_square, matrix_rate, decay_rate)
    value_update = adam_step(
        value_weight, reduced[2], value_moment, value_square, matrix_rate, decay_rate
    )
    output_update = adam_step(
        output_weight, reduced[3], output_moment, output_square, matrix_rate, decay_rate
    )
    gate_up_update = adam_step(
        gate_up_weight, reduced[4], gate_up_moment, gate_up_square, matrix_rate, decay_rate
    )
    down_update = adam_step(
        down_weight, reduced[5], down_moment, down_square, matrix_rate, decay_rate
    )
    gains_update = adam_step(norm_gains, gains_grad, gains_moment, gains_square, gain_rate, 0.0)
    return (
        block_out,
        input_grad,
        reduced[0],
        query_update[0],
        query_update[1],
        query_update[2],
        reduced[1],
        key_update[0],
        key_update[1],
        key_update[2],
        reduced[2],
        value_update[0],
        value_update[1],
        value_update[2],
        reduced[3],
        output_update[0],
        output_update[1],
        output_update[2],
        reduced[4],
        gate_up_update[0],
        gate_up_update[1],
        gate_up_update[2],
        reduced[5],
        down_update[0],
        down_update[1],
        down_update[2],
        gains_grad,
        gains_update[0],
        gains_update[1],
        gains_update[2],
    )


def solution(mesh):
    in_specs = (
        P(("dp", "row", "col"), None),
        P(("dp", "row", "col"), None),
        P(("dp", "row", "col")),
        P(("dp", "row", "col")),
        P("row", "col"),
        P("row", "col"),
        P("row", "col"),
        P("row", "col"),
        P(None, "row", "col"),
        P("row", "col"),
        P(),
        P("row", "col"),
        P("row", "col"),
        P("row", "col"),
        P("row", "col"),
        P(None, "row", "col"),
        P("row", "col"),
        P(),
        P("row", "col"),
        P("row", "col"),
        P("row", "col"),
        P("row", "col"),
        P(None, "row", "col"),
        P("row", "col"),
        P(),
    )
    out_specs = (
        P(("dp", "row", "col"), None),
        P(("dp", "row", "col"), None),
        P("row", "col"),
        P("row", "col"),
        P("row", "col"),
        P("row", "col"),
        P("row", "col"),
        P("row", "col"),
        P("row", "col"),
        P("row", "col"),
        P("row", "col"),
        P("row", "col"),
        P("row", "col"),
        P("row", "col"),
        P("row", "col"),
        P("row", "col"),
        P("row", "col"),
        P("row", "col"),
        P(None, "row", "col"),
        P(None, "row", "col"),
        P(None, "row", "col"),
        P(None, "row", "col"),
        P("row", "col"),
        P("row", "col"),
        P("row", "col"),
        P("row", "col"),
        P(),
        P(),
        P(),
        P(),
    )
    return jax.shard_map(shards, mesh=mesh, in_specs=in_specs, out_specs=out_specs, check_vma=False)
```

profile of v0, /device:TPU:0, one launch (start us, length us, event | category | flops | bytes accessed | tf_op | source)
XLA Modules:
  0.0 1015.4 jit_solution(927677411775391463)
XLA Ops:
  18.1 12.4 %all-gather.6 = bf16[8,480,80]{1,2,0:T(8,128)(2,1)S(1)} all-gather(bf16[1,480,80]{1,2,0:T(8,128)(2,1)S(1)} %convert_bitcast_fusion.7), channel_id=3, replica_groups=mesh['dp'=4,'row'=2,'col'=4] {'row','col'}, dimensions={0}, use_global_device_ids=true | all-gather | bytes 691200 | tf_op jit(solution)/shard_map/all_gather | solution.py:221
  30.5 12.8 %all-gather.7 = bf16[8,480,80]{1,2,0:T(8,128)(2,1)S(1)} all-gather(bf16[1,480,80]{1,2,0:T(8,128)(2,1)S(1)} %convert_bitcast_fusion.6), channel_id=4, replica_groups=mesh['dp'=4,'row'=2,'col'=4] {'row','col'}, dimensions={0}, use_global_device_ids=true | all-gather | bytes 691200 | tf_op jit(solution)/shard_map/all_gather | solution.py:222
  53.7 20.2 %all-gather.13.cloned.1.call-done = bf16[3840,240]{1,0:T(8,128)(2,1)} async-done(((bf16[480,240]{1,0:T(8,128)(2,1)}), bf16[3840,240]{1,0:T(8,128)(2,1)}) %all-gather.13.cloned.1.call-update) | async-done | bytes 1843216 | tf_op jit(solution)/shard_map/all_gather | solution.py:220
  84.1 72.5 %while.26 = (s32[]{:T(128)}, bf16[5,3,1024,64]{2,3,1,0:T(8,128)(2,1)}, f32[5,3,1024]{2,1,0:T(4,128)}, s32[5,1024]{1,0:T(8,128)S(1)}, bf16[5,3,1024,64]{2,3,1,0:T...) while((s32[]{:T(128)}, bf16[5,3,1024,64]{2,3,1,0:T(8,128)(2,1)}, ...), condition=%wide.region_4.5_spmd, body=%wide.region_1.4_spmd.sunk | while | flops 846394368 | bytes 47303284 | solution.py:254
  92.8 5.7 fusion.168
  107.3 5.7 fusion.168
  121.7 5.7 fusion.168
  136.1 5.7 fusion.168
  150.7 5.7 fusion.168
  156.6 5.1 multiply_reduce_fusion.2
  164.1 7.9 copy.194
  172.0 9.0 dot_general.136
  181.0 17.6 %convolution_bitcast_fusion.1 = f32[2,1024,4,640]{1,3,0,2:T(8,128)} fusion(bf16[1024,2,480,1,1]{0,2,4,3,1:T(8,128)(2,1)S(1)} %bitcast.435, bf16[2,4,2,480,640]{4,3,2,1,0:T(8,128)(2,1)} %bitcast.406), kind=kOutput, calls=%fused_computation.82 | convolution fusion | flops 10066329600 | bytes 32768000 | tf_op jit(solution)/shard_map/tra,rcgab->gtcb/dot_general | solution.py:262
  198.6 30.1 %fusion.106 = (f32[1,1024,4,640]{1,3,0,2:T(8,128)}, bf16[1,1024,4,640]{1,3,0,2:T(8,128)(2,1)}, f32[1,1024,4,640]{1,3,0,2:T(8,128)}) fusion(f32[2,1024,4,640]{1,3,0,2:T(8,128)} %convolution_bitcast_fusion.1), kind=kLoop, calls=%fused_computation.184 | loop fusion | flops 13107200 | bytes 47185920 | tf_op jit(solution)/shard_map/slice | solution.py:265
  228.7 11.5 %copy.148 = f32[1024,2560]{1,0:T(8,128)} copy(f32[1024,2560]{0,1:T(8,128)} %bitcast.399) | data formatting | bytes 20971520 | tf_op jit(solution)/shard_map/squeeze | solution.py:266
  240.2 11.6 %copy.149 = f32[1024,2560]{1,0:T(8,128)} copy(f32[1024,2560]{0,1:T(8,128)} %bitcast.398) | data formatting | bytes 20971520 | tf_op jit(solution)/shard_map/squeeze | solution.py:265
  251.9 17.5 %fusion.62 = (bf16[1024,2560]{1,0:T(8,128)(2,1)}, bf16[1024,2560]{1,0:T(8,128)(2,1)}) fusion(f32[1024,2560]{1,0:T(8,128)} %copy.149, f32[1024,2560]{1,0:T(8,128)} %copy.148, bf16[1024,2,480]{0,2,1:T(8,128)(2,1)S(1)} %bitcast.409, bf16[2560,480,2]{0,1,2:T(8,128)(2,1)} %dot_general.136), kind=kOutput, calls=%fused_computation.73 | convolution fusion | flops 5067243520 | bytes 38338560 | tf_op jit(solution)/shard_map/tra,rcaf->tcf/dot_general | solution.py:275
  269.3 9.8 stack.18
  279.1 5.5 copy_dynamic-update-slice_fusion.1
  284.6 9.8 stack.19
  294.4 8.8 copy.154
  303.2 5.7 copy_dynamic-update-slice_fusion
  308.8 17.1 %fusion.81 = (f32[960]{0:T(1024)}, f32[1024]{0:T(1024)S(1)}, f32[1024,960,1,1]{0,1,3,2:T(8,128)S(1)}) fusion(f32[1024,960]{0,1:T(8,128)S(1)} %copy-done.2, f32[1024]{0:T(1024)S(1)} %copy-done.59, f32[960]{0:T(1024)S(1)} %bitcast.451, bf16[2,1024,4,640]{3,1,0,2:T(8,128)(2,1)} %copy_dynamic-update-slice_fusion, bf16[960,640,4,2]{1,0,3,2:T(8,128)(2,1)} %bitcast.408), kind=kOutput, calls=%fused_computation.105 | convolution fusion | flops 10072225792 | bytes 28196352 | tf_op jit(solution)/shard_map/gtcb,rcgab->tra/dot_general | solution.py:289
  331.2 149.7 %while.27 = (s32[]{:T(128)}, f32[5,3,1024,64]{2,3,1,0:T(8,128)}, f32[5,1024,64]{1,2,0:T(8,128)}, bf16[5,1024,64]{1,2,0:T(8,128)(2,1)S(1)}, s32[5,1024]{1,0:T(8,1...) while((s32[]{:T(128)}, f32[5,3,1024,64]{2,3,1,0:T(8,128)}, ...), condition=%wide.region_9.10_spmd, body=%wide.region_7.9_spmd.sunk | while | flops 2063856640 | bytes 101954672 | solution.py:298
  336.6 7.5 multiply_reduce_fusion.4
  344.1 6.9 multiply_convert_fusion.4
  366.5 7.5 multiply_reduce_fusion.4
  374.0 6.9 multiply_convert_fusion.4
  396.4 7.5 multiply_reduce_fusion.4
  403.9 6.9 multiply_convert_fusion.4
  426.2 7.5 multiply_reduce_fusion.4
  433.8 6.9 multiply_convert_fusion.4
  456.1 7.5 multiply_reduce_fusion.4
  463.6 6.9 multiply_convert_fusion.4
  505.7 5.8 convolution_bitcast_fusion.3
  511.5 5.1 copy.162
  518.2 7.3 fusion.83
  531.5 16.8 %fusion.63 = f32[2,4,2,480,640]{4,3,0,1,2:T(8,128)} fusion(bf16[1024,2,480,1,1]{0,2,1,4,3:T(8,128)(2,1)S(1)} %bitcast.436, bf16[2,1024,4,640]{3,1,0,2:T(8,128)(2,1)} %copy_dynamic-update-slice_fusion), kind=kOutput, calls=%fused_computation.83 | convolution fusion | flops 10066329600 | bytes 32112640 | tf_op jit(solution)/shard_map/tra,gtcb->rcgab/dot_general | solution.py:286
  548.3 15.3 %copy.164 = f32[2,4,2,480,640]{4,3,2,1,0:T(8,128)} copy(f32[2,4,2,480,640]{4,3,0,1,2:T(8,128)} %fusion.63) | data formatting | bytes 39321600 | tf_op jit(solution)/shard_map/tra,gtcb->rcgab/transpose | solution.py:286
  574.7 5.5 copy.145
  588.8 39.8 %psum.55 = f32[2,960]{1,0:T(2,128)S(1)} all-reduce(f32[2,960]{1,0:T(2,128)S(1)} %pad_maximum_fusion), channel_id=1, replica_groups=mesh['dp'=4,'row'=2,'col'=4] {'dp','row','col'}, use_global_device_ids=true, to_apply=%region_25.26 | all-reduce | flops 1920 | bytes 15360 | tf_op jit(solution)/shard_map/psum | solution.py:347
  634.2 39.1 %reduce-scatter.13.cloned.1.call-done = f32[1,480,240]{2,1,0:T(8,128)} async-done(((f32[8,480,240]{2,1,0:T(8,128)}), f32[1,480,240]{2,1,0:T(8,128)}) %reduce-scatter.13.cloned.1.call-update) | async-done | bytes 460816 | tf_op jit(solution)/shard_map/reduce_scatter | solution.py:329
  675.1 80.1 %reduce-scatter.17.cloned.1.call-done = f32[1,480,640]{2,1,0:T(8,128)} async-done(((f32[8,480,640]{2,1,0:T(8,128)}), f32[1,480,640]{2,1,0:T(8,128)}) %reduce-scatter.17.cloned.1.call-update) | async-done | bytes 1228816 | tf_op jit(solution)/shard_map/reduce_scatter | solution.py:331
  757.4 131.0 %reduce-scatter.15.cloned.1.call-done = f32[1,2,480,640]{3,2,1,0:T(8,128)} async-done(((f32[8,2,480,640]{3,2,1,0:T(8,128)}), f32[1,2,480,640]{3,2,1,0:T(8,128)}) %reduce-scatter.15.cloned.1.call-update) | async-done | bytes 2457616 | tf_op jit(solution)/shard_map/reduce_scatter | solution.py:330
  891.3 7.1 fusion.76
  898.4 9.8 fusion.82
  908.2 86.3 %all-reduce.3.cloned.1.call-done = (bf16[480,240]{1,0:T(8,128)(2,1)}, bf16[480,80]{0,1:T(8,128)(2,1)}, bf16[480,80]{0,1:T(8,128)(2,1)}, bf16[480,240]{1,0:T(8,12...) async-done(((bf16[480,240]{1,0:T(8,128)(2,1)}, bf16[480,80]{0,1:T(8,128)(2,1)}, bf16[480,80]{0,1:T(8,128)(2,1)}, bf16[480,240]{1,0:T(8,128)(2,1)}, ...) | async-done | bytes 2457616 | tf_op jit(solution)/shard_map/psum | solution.py:340
  994.6 7.2 multiply_subtract_fusion
  (323 shorter events, 229.6 us)
Async XLA Ops:
  7.2 40.9 %all-gather.15.cloned.1.call-start = ((), (), s32[]{:S(2)}) async-start(), calls=%async_computation.13 | async-start | bytes 2211840 | tf_op jit(solution)/shard_map/all_gather | solution.py:223
  9.0 64.9 %all-gather.13.cloned.1.call-start = ((), (), s32[]{:S(2)}) async-start(), calls=%async_computation.12 | async-start | bytes 2211840 | tf_op jit(solution)/shard_map/all_gather | solution.py:220
  10.8 5.6 copy-start.4
  10.8 153.2 %all-gather.19.cloned.1.call-start = ((), (), s32[]{:S(2)}) async-start(), calls=%async_computation.15 | async-start | bytes 5529600 | tf_op jit(solution)/shard_map/all_gather | solution.py:225
  13.2 4.8 copy-start.79
  13.2 4.8 copy-start.40
  13.2 17.3 %copy-start.42 = (f32[480,80]{0,1:T(8,128)S(1)}, f32[480,80]{0,1:T(8,128)}, u32[]{:S(2)}) copy-start(f32[480,80]{0,1:T(8,128)} %param.35) | copy-start | bytes 460804
  13.2 167.7 %all-gather.17.cloned.1.call-start = ((), (), s32[]{:S(2)}) async-start(), calls=%async_computation.14 | async-start | bytes 11059200 | tf_op jit(solution)/shard_map/all_gather | solution.py:224
  16.3 613.0 %reduce-scatter.9.cloned.1.call-start = ((), (), s32[]{:S(2)}) async-start(), calls=%async_computation.7 | async-start | bytes 1474560 | tf_op jit(solution)/shard_map/reduce_scatter | solution.py:327
  17.4 27.9 %copy-start.68 = (f32[1024]{0:T(1024)}, f32[1024]{0:T(1024)S(1)}, u32[]{:S(2)}) copy-start(f32[1024]{0:T(1024)S(1)} %get-tuple-element.220) | copy-start | bytes 12292
  18.1 27.3 %copy-start.70 = (f32[1,960]{1,0:T(1,128)}, f32[1,960]{1,0:T(1,128)S(1)}, u32[]{:S(2)}) copy-start(f32[1,960]{1,0:T(1,128)S(1)} %get-tuple-element.216) | copy-start | bytes 11524
  30.5 14.8 %copy-start.21 = (bf16[8,480,80]{1,2,0:T(8,128)(2,1)}, bf16[8,480,80]{1,2,0:T(8,128)(2,1)S(1)}, u32[]{:S(2)}) copy-start(bf16[8,480,80]{1,2,0:T(8,128)(2,1)S(1)} %all-gather.6) | copy-start | bytes 1843204
  53.7 24.2 %copy-start.29 = (bf16[1024,960]{0,1:T(8,128)(2,1)S(1)}, bf16[1024,960]{0,1:T(8,128)(2,1)}, u32[]{:S(2)}) copy-start(bf16[1024,960]{0,1:T(8,128)(2,1)} %copy-done.28) | copy-start | bytes 5898244
  156.6 5.2 copy-start.51
  156.6 7.1 copy-start.61
  164.0 16.9 %copy-start.31 = (bf16[1024,960]{0,1:T(8,128)(2,1)}, bf16[1024,960]{0,1:T(8,128)(2,1)S(1)}, u32[]{:S(2)}) copy-start(bf16[1024,960]{0,1:T(8,128)(2,1)S(1)} %multiply_convert_fusion.2) | copy-start | bytes 5898244
  240.2 11.7 %copy-start.8 = (bf16[1024,960]{0,1:T(8,128)(2,1)S(1)}, bf16[1024,960]{0,1:T(8,128)(2,1)}, u32[]{:S(2)}) copy-start(bf16[1024,960]{0,1:T(8,128)(2,1)} %param.30) | copy-start | bytes 5898244
  303.2 5.7 copy-start.2
  303.2 5.7 copy-start.59
  303.2 5.7 copy-start.62
  308.8 17.1 %copy-start.64 = (f32[1024]{0:T(1024)S(1)}, f32[1024]{0:T(1024)}, u32[]{:S(2)}) copy-start(f32[1024]{0:T(1024)} %get-tuple-element.221) | copy-start | bytes 12292
  331.2 149.7 %copy-start.15 = (f32[1024,32]{0,1:T(8,128)S(1)}, f32[1024,32]{0,1:T(8,128)}, u32[]{:S(2)}) copy-start(f32[1024,32]{0,1:T(8,128)} %copy-done.13) | copy-start | bytes 393220
  331.2 149.7 %copy-start.18 = (f32[1024,32]{0,1:T(8,128)S(1)}, f32[1024,32]{0,1:T(8,128)}, u32[]{:S(2)}) copy-start(f32[1024,32]{0,1:T(8,128)} %copy-done.16) | copy-start | bytes 393220
  480.9 5.7 copy-start.24
  486.4 144.4 %reduce-scatter.11.cloned.1.call-start = ((), (), s32[]{:S(2)}) async-start(), calls=%async_computation.8 | async-start | bytes 1474560 | tf_op jit(solution)/shard_map/reduce_scatter | solution.py:328
  490.3 142.1 %reduce-scatter.7.cloned.1.call-start = ((), (), s32[]{:S(2)}) async-start(), calls=%async_computation.6 | async-start | bytes 4423680 | tf_op jit(solution)/shard_map/reduce_scatter | solution.py:326
  490.3 4.5 copy-start.30
  504.2 169.1 %reduce-scatter.13.cloned.1.call-start = ((), (), s32[]{:S(2)}) async-start(), calls=%async_computation.9 | async-start | bytes 4423680 | tf_op jit(solution)/shard_map/reduce_scatter | solution.py:329
  516.7 238.5 %reduce-scatter.17.cloned.1.call-start = ((), (), s32[]{:S(2)}) async-start(), calls=%async_computation.11 | async-start | bytes 11059200 | tf_op jit(solution)/shard_map/reduce_scatter | solution.py:331
  530.0 358.4 %reduce-scatter.15.cloned.1.call-start = ((), (), s32[]{:S(2)}) async-start(), calls=%async_computation.10 | async-start | bytes 22118400 | tf_op jit(solution)/shard_map/reduce_scatter | solution.py:330
  563.6 11.0 %copy-start.10 = (bf16[3840,240]{1,0:T(8,128)(2,1)S(1)}, bf16[3840,240]{1,0:T(8,128)(2,1)}, u32[]{:S(2)}) copy-start(bf16[3840,240]{1,0:T(8,128)(2,1)} %all-gather.13.cloned.1.call-done) | copy-start | bytes 5529604
  563.6 430.9 %all-reduce.3.cloned.1.call-start = ((), (), s32[]{:S(2)}) async-start(), calls=%async_computation.16 | async-start | bytes 4997120 | tf_op jit(solution)/shard_map/psum | solution.py:340
  583.9 4.8 copy-start.80
  583.9 44.7 %copy-start.73 = (f32[2,960]{1,0:T(2,128)S(1)}, f32[2,960]{1,0:T(2,128)}, u32[]{:S(2)}) copy-start(f32[2,960]{1,0:T(2,128)} %param.39) | copy-start | bytes 23044
  583.9 44.7 %copy-start.76 = (f32[2,960]{1,0:T(2,128)S(1)}, f32[2,960]{1,0:T(2,128)}, u32[]{:S(2)}) copy-start(f32[2,960]{1,0:T(2,128)} %param.53) | copy-start | bytes 23044
  583.9 44.7 %copy-start.77 = (f32[2,960]{1,0:T(2,128)S(1)}, f32[2,960]{1,0:T(2,128)}, u32[]{:S(2)}) copy-start(f32[2,960]{1,0:T(2,128)} %param.46) | copy-start | bytes 23044
  628.6 262.6 %copy-start.74 = (f32[2,960]{1,0:T(2,128)}, f32[2,960]{1,0:T(2,128)S(1)}, u32[]{:S(2)}) copy-start(f32[2,960]{1,0:T(2,128)S(1)} %psum.55) | copy-start | bytes 23044
  675.0 216.2 %copy-start.60 = (f32[1024]{0:T(1024)S(1)}, f32[1024]{0:T(1024)}, u32[]{:S(2)}) copy-start(f32[1024]{0:T(1024)} %copy-done.58) | copy-start | bytes 12292
  675.0 216.2 %copy-start.63 = (f32[1,960]{1,0:T(1,128)S(1)}, f32[1,960]{1,0:T(1,128)}, u32[]{:S(2)}) copy-start(f32[1,960]{1,0:T(1,128)} %get-tuple-element.215) | copy-start | bytes 11524
  675.0 216.2 %copy-start.65 = (f32[1024]{0:T(1024)S(1)}, f32[1024]{0:T(1024)}, u32[]{:S(2)}) copy-start(f32[1024]{0:T(1024)} %get-tuple-element.221) | copy-start | bytes 12292
  675.0 216.2 %copy-start.67 = (f32[1024]{0:T(1024)S(1)}, f32[1024]{0:T(1024)}, u32[]{:S(2)}) copy-start(f32[1024]{0:T(1024)} %copy-done.66) | copy-start | bytes 12292
  675.1 216.2 %copy-start.75 = (f32[1024]{0:T(1024)S(1)}, f32[1024]{0:T(1024)}, u32[]{:S(2)}) copy-start(f32[1024]{0:T(1024)} %get-tuple-element.219) | copy-start | bytes 12292
  891.3 7.1 copy-start.3
  898.4 96.1 %copy-start.7 = (f32[2,480,640]{2,1,0:T(8,128)S(1)}, f32[2,480,640]{2,1,0:T(8,128)}, u32[]{:S(2)}) copy-start(f32[2,480,640]{2,1,0:T(8,128)} %param.37) | copy-start | bytes 7372804
  994.5 7.2 copy-start.12
  994.5 7.2 copy-start.38
  994.5 7.2 copy-start.39
  994.5 7.2 copy-start.44
  (48 other events, 133.7 us)
Sparse Core Ops, SparseCore 0:
  10.5 33.2 all-gather.14
  46.3 27.5 all-gather.12
  76.4 39.7 all-gather.18
  118.5 60.4 all-gather.16
  486.5 37.3 reduce-scatter.8
  527.6 37.2 reduce-scatter.10
  568.5 50.7 reduce-scatter.6
  623.2 50.0 reduce-scatter.12
  676.9 78.2 reduce-scatter.16
  758.7 129.5 reduce-scatter.14
  892.4 102.1 all-reduce.2
where the time goes:
time: 1030 us; the launch traced here: 1020 us
  waiting for transfers between devices  357 us (35%)
  matrix products  272 us (26%)
  local copies, waits for them, and re-layouts  157 us (15%)
  other arithmetic  147 us (14%)
  blocking collectives  65.1 us (6%)
  between operations  15.2 us (1%)
    reduce_scatter x1, waiting for transfers between devices, shards(): lax.psum_scatter(gate_up_block, ('row', 'col'), scatter_dimension=0, tile...  131 us
    psum x1, waiting for transfers between devices, shards(): lax.psum(query_sum.astype(jnp.bfloat16), 'dp').astype(jnp.float32)  86.3 us
    reduce_scatter x1, waiting for transfers between devices, shards(): lax.psum_scatter(down_block, ('row', 'col'), scatter_dimension=0, tiled=T...  80.1 us
    psum x1, blocking collectives, shards(): gains_grad = lax.psum(jnp.stack([gain_one, gain_two]), ('dp', 'row', 'col'))  39.8 us
    reduce_scatter x1, waiting for transfers between devices, shards(): lax.psum_scatter(output_block, ('row', 'col'), scatter_dimension=0, tiled...  39.1 us
    dot_general x5, matrix products, head_backward(): jnp.einsum('gqd,sd->gqs', out_grad, value_rows, preferred_element_type=jn...  37.6 us
    convert_element_type x5, other arithmetic, head_backward(): score_grad = (chances * (chance_grad - centre)).astype(jnp.bfloat16)  34.7 us
    dot_general x10, matrix products, scaled_scores(): jnp.einsum('gqd,sd->gqs', queries, key_rows, preferred_element_type=jnp.f...  32.4 us
  transfers between devices with their start and end apart: 11, of which 5 were waited for; matrix products, arithmetic and copies ran while one was open for 24% of the time, Pallas kernels for 0%

commit v1 on v0

v1 whole, which is shorter than its diff:
```python
import math

import jax
import jax.numpy as jnp
from jax import lax
from jax.experimental import pallas as pl
from jax.experimental.pallas import tpu as pltpu
from jax.sharding import PartitionSpec as P

HEADS = 15
KV_HEADS = 5
HEAD_DIM = 64
SEQ = 1024
STEP = 10
GROUP = HEADS // KV_HEADS
TILE = 256


norm_eps = 1e-05
rope_base = 100000.0
beta_one = 0.9
beta_two = 0.95
adam_eps = 1e-08
decay_rate = 0.1
matrix_rate = 0.1
gain_rate = 1.0
masked_fill = -1000000000.0


def rope_tables(positions):
    ladder = jnp.arange(HEAD_DIM // 2, dtype=jnp.float32) * (2.0 / HEAD_DIM)
    frequency = jnp.exp(ladder * -math.log(rope_base))
    angles = frequency[:, None] * positions.astype(jnp.float32)[None, :]
    return (jnp.cos(angles), jnp.sin(angles))


def rotate(values, cos_table, sine_table):
    half_dim = HEAD_DIM // 2
    upper = values[:half_dim]
    lower = values[half_dim:]
    return jnp.concatenate(
        [upper * cos_table - lower * sine_table, lower * cos_table + upper * sine_table], axis=0
    )


def dot(left, right, dims=((1,), (0,))):
    return lax.dot_general(left, right, (dims, ((), ())), preferred_element_type=jnp.float32)


def fill_bias(bias, seg_row, seg_col):
    @pl.when(pl.program_id(0) == 0)
    def _():
        for start in range(0, SEQ, TILE):
            size = start + TILE
            earlier = lax.broadcasted_iota(jnp.int32, (size, TILE), 0)
            later = lax.broadcasted_iota(jnp.int32, (size, TILE), 1) + start
            same = seg_col[:size] == seg_row[:, start:size]
            bias[:size, start:size] = jnp.where((earlier <= later) & same, 0.0, masked_fill)


def attend_kernel(
    q_ref, k_ref, v_ref, cos_ref, sin_ref, seg_row, seg_col, low_ref, out_ref, log_ref, bias
):
    fill_bias(bias, seg_row, seg_col)
    pair = pl.program_id(0)
    cos_table = cos_ref[...]
    sine_table = sin_ref[...]
    keys = rotate(k_ref[...], cos_table, sine_table).astype(jnp.bfloat16)
    values = v_ref[...].astype(jnp.bfloat16)
    query_width = HEADS * HEAD_DIM
    kv_width = KV_HEADS * HEAD_DIM
    place = pl.multiple_of(pair * HEAD_DIM, HEAD_DIM)
    low_ref[pl.ds(query_width + place, HEAD_DIM), :] = keys
    low_ref[pl.ds(query_width + kv_width + place, HEAD_DIM), :] = values
    key_rows = keys.T
    for head in range(GROUP):
        rows = slice(head * HEAD_DIM, (head + 1) * HEAD_DIM)
        queries = rotate(q_ref[rows, :], cos_table, sine_table).astype(jnp.bfloat16)
        low_ref[pl.ds(pl.multiple_of((pair * GROUP + head) * HEAD_DIM, HEAD_DIM), HEAD_DIM), :] = (
            queries
        )
        scaled = queries * HEAD_DIM ** (-0.5)
        for start in range(0, SEQ, TILE):
            size = start + TILE
            scores = dot(key_rows[:size], scaled[:, start:size]) + bias[:size, start:size]
            summit = jnp.max(scores, axis=0, keepdims=True)
            powers = jnp.exp(scores - summit)
            totals = jnp.sum(powers, axis=0, keepdims=True)
            blended = dot(values[:, :size], powers.astype(jnp.bfloat16)) / totals
            out_ref[rows, start:size] = blended.astype(jnp.bfloat16)
            log_ref[0, head : head + 1, start:size] = summit + jnp.log(totals)


def attend_back_kernel(
    q_ref,
    k_ref,
    v_ref,
    grad_ref,
    log_ref,
    cos_ref,
    sin_ref,
    seg_row,
    seg_col,
    out_ref,
    bias,
    key_total,
    value_total,
):
    fill_bias(bias, seg_row, seg_col)
    pair = pl.program_id(0)
    cos_table = cos_ref[...]
    sine_table = -sin_ref[...]
    scale = HEAD_DIM ** (-0.5)
    keys = k_ref[...]
    key_rows = keys.T
    value_rows = v_ref[...].T
    key_total[...] = jnp.zeros_like(key_total)
    value_total[...] = jnp.zeros_like(value_total)
    for head in range(GROUP):
        rows = slice(head * HEAD_DIM, (head + 1) * HEAD_DIM)
        queries = q_ref[rows, :]
        scaled = queries * scale
        query_rows = scaled.T
        incoming = grad_ref[rows, :]
        incoming_rows = incoming.T
        parts = []
        for start in range(0, SEQ, TILE):
            size = start + TILE
            scores = dot(key_rows[:size], scaled[:, start:size]) + bias[:size, start:size]
            chances = jnp.exp(scores - log_ref[0, head : head + 1, start:size])
            chance_grad = dot(value_rows[:size], incoming[:, start:size])
            centre = jnp.sum(chances * chance_grad, axis=0, keepdims=True)
            score_grad = (chances * (chance_grad - centre)).astype(jnp.bfloat16)
            parts.append(dot(keys[:, :size], score_grad) * scale)
            key_total[:size] += dot(score_grad, query_rows[start:size])
            value_total[:size] += dot(chances.astype(jnp.bfloat16), incoming_rows[start:size])
        query_grad = rotate(jnp.concatenate(parts, axis=1), cos_table, sine_table)
        out_ref[pl.ds(pl.multiple_of((pair * GROUP + head) * HEAD_DIM, HEAD_DIM), HEAD_DIM), :] = (
            query_grad.astype(jnp.bfloat16)
        )
    query_width = HEADS * HEAD_DIM
    kv_width = KV_HEADS * HEAD_DIM
    place = pl.multiple_of(pair * HEAD_DIM, HEAD_DIM)
    key_grad = rotate(key_total[...].T, cos_table, sine_table)
    out_ref[pl.ds(query_width + place, HEAD_DIM), :] = key_grad.astype(jnp.bfloat16)
    out_ref[pl.ds(query_width + kv_width + place, HEAD_DIM), :] = (
        value_total[...].T.astype(jnp.bfloat16)
    )


def whole_spec(*shape):
    return pl.BlockSpec(shape, lambda step: (0,) * len(shape))


def head_specs():
    return [
        pl.BlockSpec((GROUP * HEAD_DIM, SEQ), lambda j: (j, 0)),
        pl.BlockSpec((HEAD_DIM, SEQ), lambda j: (HEADS + j, 0)),
        pl.BlockSpec((HEAD_DIM, SEQ), lambda j: (HEADS + KV_HEADS + j, 0)),
    ]


def attend(projected, cos_table, sine_table, segments):
    half_dim = HEAD_DIM // 2
    width = projected.shape[0]
    return pl.pallas_call(
        attend_kernel,
        grid=(KV_HEADS,),
        in_specs=head_specs()
        + [
            whole_spec(half_dim, SEQ),
            whole_spec(half_dim, SEQ),
            whole_spec(1, SEQ),
            whole_spec(SEQ, 1),
        ],
        out_specs=[
            whole_spec(width, SEQ),
            pl.BlockSpec((GROUP * HEAD_DIM, SEQ), lambda j: (j, 0)),
            pl.BlockSpec((1, GROUP, SEQ), lambda j: (j, 0, 0)),
        ],
        out_shape=[
            jax.ShapeDtypeStruct((width, SEQ), jnp.bfloat16),
            jax.ShapeDtypeStruct((HEADS * HEAD_DIM, SEQ), jnp.bfloat16),
            jax.ShapeDtypeStruct((KV_HEADS, GROUP, SEQ), jnp.float32),
        ],
        scratch_shapes=[pltpu.VMEM((SEQ, SEQ), jnp.float32)],
        compiler_params=pltpu.CompilerParams(vmem_limit_bytes=48 << 20),
        cost_estimate=pl.CostEstimate(
            flops=20 * SEQ * SEQ * HEADS * HEAD_DIM,
            bytes_accessed=16 << 20,
            transcendentals=HEADS * SEQ * SEQ,
        ),
        name="attend",
    )(
        projected,
        projected,
        projected,
        cos_table,
        sine_table,
        segments.reshape(1, SEQ),
        segments.reshape(SEQ, 1),
    )


def attend_back(low, blended_grad, log_totals, cos_table, sine_table, segments):
    half_dim = HEAD_DIM // 2
    width = low.shape[0]
    return pl.pallas_call(
        attend_back_kernel,
        grid=(KV_HEADS,),
        in_specs=head_specs()
        + [
            pl.BlockSpec((GROUP * HEAD_DIM, SEQ), lambda j: (j, 0)),
            pl.BlockSpec((1, GROUP, SEQ), lambda j: (j, 0, 0)),
            whole_spec(half_dim, SEQ),
            whole_spec(half_dim, SEQ),
            whole_spec(1, SEQ),
            whole_spec(SEQ, 1),
        ],
        out_specs=whole_spec(width, SEQ),
        out_shape=jax.ShapeDtypeStruct((width, SEQ), jnp.bfloat16),
        scratch_shapes=[
            pltpu.VMEM((SEQ, SEQ), jnp.float32),
            pltpu.VMEM((SEQ, HEAD_DIM), jnp.float32),
            pltpu.VMEM((SEQ, HEAD_DIM), jnp.float32),
        ],
        compiler_params=pltpu.CompilerParams(vmem_limit_bytes=48 << 20),
        cost_estimate=pl.CostEstimate(
            flops=60 * SEQ * SEQ * HEADS * HEAD_DIM,
            bytes_accessed=16 << 20,
            transcendentals=HEADS * SEQ * SEQ,
        ),
        name="attend_back",
    )(
        low,
        low,
        low,
        blended_grad,
        log_totals,
        cos_table,
        sine_table,
        segments.reshape(1, SEQ),
        segments.reshape(SEQ, 1),
    )


def mlp_kernel(
    normed_ref,
    normed_turned,
    back_ref,
    back_turned,
    pair_ref,
    down_ref,
    out_ref,
    grad_ref,
    pair_out,
    down_out,
    hidden_keep,
    gate_keep,
    up_keep,
):
    first = pl.program_id(0) == 0
    height = pair_ref.shape[0] * pair_ref.shape[3]
    width = pair_ref.shape[4]
    token_count = normed_ref.shape[0]

    @pl.when(first)
    def _():
        out_ref[...] = jnp.zeros_like(out_ref)
        grad_ref[...] = jnp.zeros_like(grad_ref)

    gate_weight = pair_ref[:, 0, 0].reshape(height, width)
    up_weight = pair_ref[:, 0, 1].reshape(height, width)
    down_weight = down_ref[:, 0].reshape(height, width)

    def forward(step, carry):
        rows = pl.ds(pl.multiple_of(step * TILE, TILE), TILE)
        normed = normed_ref[rows, :]
        gate_pre = dot(normed, gate_weight)
        up_pre = dot(normed, up_weight)
        hidden_grad = dot(back_ref[rows, :], down_weight)
        sigmoid_gate = 1.0 / (1.0 + jnp.exp(-gate_pre))
        silu_gate = gate_pre * sigmoid_gate
        hidden = (silu_gate * up_pre).astype(jnp.bfloat16)
        gate_grad = (
            hidden_grad * up_pre * sigmoid_gate * (1.0 + gate_pre * (1.0 - sigmoid_gate))
        ).astype(jnp.bfloat16)
        up_grad = (hidden_grad * silu_gate).astype(jnp.bfloat16)
        hidden_keep[rows, :] = hidden
        gate_keep[rows, :] = gate_grad
        up_keep[rows, :] = up_grad
        out_ref[rows, :] += dot(hidden, down_weight, ((1,), (1,)))
        grad_ref[rows, :] += dot(gate_grad, gate_weight, ((1,), (1,))) + dot(
            up_grad, up_weight, ((1,), (1,))
        )
        return carry

    lax.fori_loop(0, token_count // TILE, forward, 0)
    block_rows = pair_ref.shape[3]
    for block in range(pair_ref.shape[0]):
        rows = slice(block * block_rows, (block + 1) * block_rows)
        left = normed_turned[rows, :]
        pair_out[block, 0, 0] = dot(left, gate_keep[...]).astype(jnp.bfloat16)
        pair_out[block, 0, 1] = dot(left, up_keep[...]).astype(jnp.bfloat16)
        down_out[block, 0] = dot(back_turned[rows, :], hidden_keep[...]).astype(jnp.bfloat16)


def mlp(normed, back, pair_grid, down_grid):
    token_count, features = normed.shape
    row_count, col_count, _, height, width = pair_grid.shape
    aligned = height % 16 == 0 and width % 128 == 0
    if not aligned:
        units = col_count * width
        pieces = units // 640
        pair_grid = pair_grid.transpose(2, 0, 3, 1, 4).reshape(1, 2, features, pieces, 640)
        pair_grid = pair_grid.transpose(0, 3, 1, 2, 4)
        down_grid = down_grid.transpose(0, 2, 1, 3).reshape(1, features, pieces, 640)
        down_grid = down_grid.transpose(0, 2, 1, 3)
    rows, cols, _, tall, wide = pair_grid.shape
    single = pl.Buffered(1)

    def fixed(*shape):
        return pl.BlockSpec(shape, lambda c: (0, 0), pipeline_mode=single)

    pair_spec = pl.BlockSpec((rows, 1, 2, tall, wide), lambda c: (0, c, 0, 0, 0))
    down_spec = pl.BlockSpec((rows, 1, tall, wide), lambda c: (0, c, 0, 0))
    outs = pl.pallas_call(
        mlp_kernel,
        grid=(cols,),
        in_specs=[
            fixed(token_count, features),
            fixed(features, token_count),
            fixed(token_count, features),
            fixed(features, token_count),
            pair_spec,
            down_spec,
        ],
        out_specs=[
            fixed(token_count, features),
            fixed(token_count, features),
            pair_spec,
            down_spec,
        ],
        out_shape=[
            jax.ShapeDtypeStruct((token_count, features), jnp.float32),
            jax.ShapeDtypeStruct((token_count, features), jnp.float32),
            jax.ShapeDtypeStruct(pair_grid.shape, jnp.bfloat16),
            jax.ShapeDtypeStruct(down_grid.shape, jnp.bfloat16),
        ],
        scratch_shapes=[pltpu.VMEM((token_count, wide), jnp.bfloat16)] * 3,
        compiler_params=pltpu.CompilerParams(vmem_limit_bytes=58 << 20),
        cost_estimate=pl.CostEstimate(
            flops=18 * token_count * features * cols * wide,
            bytes_accessed=64 << 20,
            transcendentals=token_count * cols * wide,
        ),
        name="mlp",
    )(normed, normed.T, back, back.T, pair_grid, down_grid)
    mlp_out, normed_grad, pair_grad, down_grad = outs
    if not aligned:
        pair_grad = pair_grad.transpose(0, 2, 3, 1, 4).reshape(
            2, row_count, height, col_count, width
        )
        pair_grad = pair_grad.transpose(1, 3, 0, 2, 4)
        down_grad = down_grad.transpose(0, 2, 1, 3).reshape(row_count, height, col_count, width)
        down_grad = down_grad.transpose(0, 2, 1, 3)
    return mlp_out, normed_grad, pair_grad, down_grad


def from_grid(stack, row_count, col_count):
    _, height, width = stack.shape
    shaped = stack.reshape(row_count, col_count, height, width).transpose(0, 2, 1, 3)
    return shaped.reshape(row_count * height, col_count * width)


def into_grid(whole, row_count, col_count):
    height = whole.shape[0] // row_count
    width = whole.shape[1] // col_count
    shaped = whole.reshape(row_count, height, col_count, width).transpose(0, 2, 1, 3)
    return shaped.reshape(row_count * col_count, height, width)


def norm_backward(inputs, inverse, scales, incoming):
    weighted = incoming * scales
    gain_part = jnp.sum(incoming * inputs * inverse, axis=0)
    input_part = inverse * weighted - inputs * inverse**3 * jnp.mean(
        weighted * inputs, axis=-1, keepdims=True
    )
    return (gain_part, input_part)


def adam_step(weight, gradient, moment, square, step_rate, decay_factor):
    moment_new = beta_one * moment + (1.0 - beta_one) * gradient
    square_new = beta_two * square + (1.0 - beta_two) * gradient * gradient
    scaled_step = (
        moment_new
        / (1.0 - beta_one**STEP)
        / (jnp.sqrt(square_new / (1.0 - beta_two**STEP)) + adam_eps)
    )
    return (moment_new, square_new, weight - step_rate * (scaled_step + decay_factor * weight))


def shards(
    hidden_in,
    cotangent,
    segment_ids,
    positions,
    query_weight,
    key_weight,
    value_weight,
    output_weight,
    gate_up_weight,
    down_weight,
    norm_gains,
    query_moment,
    key_moment,
    value_moment,
    output_moment,
    gate_up_moment,
    down_moment,
    gains_moment,
    query_square,
    key_square,
    value_square,
    output_square,
    gate_up_square,
    down_square,
    gains_square,
):
    row_count = lax.axis_size("row")
    col_count = lax.axis_size("col")
    query_part = query_weight.shape[1]
    key_part = key_weight.shape[1]
    cuts = (query_part, query_part + key_part, query_part + 2 * key_part)
    query_width = HEADS * HEAD_DIM
    kv_width = KV_HEADS * HEAD_DIM

    def gather(block):
        return lax.all_gather(block[None], ("row", "col"), axis=0, tiled=True)

    def scatter(stack):
        return lax.psum_scatter(stack, ("row", "col"), scatter_dimension=0, tiled=True)[0]

    def total(part):
        return lax.psum(part, "dp").astype(jnp.float32)

    first_stack = gather(
        jnp.concatenate([query_weight, key_weight, value_weight, output_weight], axis=1).astype(
            jnp.bfloat16
        )
    )
    gate_up_stack = gather(gate_up_weight.astype(jnp.bfloat16))
    down_stack = gather(down_weight.astype(jnp.bfloat16))
    first_low = jnp.concatenate(
        [
            from_grid(first_stack[:, :, : cuts[0]], row_count, col_count),
            from_grid(first_stack[:, :, cuts[0] : cuts[1]], row_count, col_count),
            from_grid(first_stack[:, :, cuts[1] : cuts[2]], row_count, col_count),
        ],
        axis=1,
    )
    output_low = from_grid(first_stack[:, :, cuts[2] :], row_count, col_count)
    gate_up_grid = gate_up_stack.reshape((row_count, col_count) + gate_up_weight.shape)
    down_grid = down_stack.reshape((row_count, col_count) + down_weight.shape)

    cos_table, sine_table = rope_tables(positions)
    inputs = hidden_in.astype(jnp.float32)
    inverse_one = lax.rsqrt(jnp.mean(inputs * inputs, axis=-1, keepdims=True) + norm_eps)
    normed_one = (inputs * inverse_one * norm_gains[0]).astype(jnp.bfloat16)
    projected = dot(first_low, normed_one, ((0,), (1,)))
    low, blended, log_totals = attend(projected, cos_table, sine_table, segment_ids)
    middle = inputs + dot(blended, output_low, ((0,), (0,)))
    inverse_two = lax.rsqrt(jnp.mean(middle * middle, axis=-1, keepdims=True) + norm_eps)
    normed_two = (middle * inverse_two * norm_gains[1]).astype(jnp.bfloat16)
    mlp_out, normed_two_grad, gate_up_block, down_block = mlp(
        normed_two, cotangent, gate_up_grid, down_grid
    )
    gate_up_part = scatter(gate_up_block.reshape(gate_up_stack.shape))
    down_part = scatter(down_block.reshape(down_stack.shape))
    block_out = (middle + mlp_out).astype(jnp.bfloat16)
    gain_two, middle_part = norm_backward(middle, inverse_two, norm_gains[1], normed_two_grad)
    middle_grad = cotangent.astype(jnp.float32) + middle_part
    middle_low = middle_grad.astype(jnp.bfloat16)
    output_block = dot(blended, middle_low, ((1,), (0,))).astype(jnp.bfloat16)
    output_part = scatter(into_grid(output_block, row_count, col_count))
    blended_grad = dot(output_low, middle_low, ((1,), (1,))).astype(jnp.bfloat16)
    projected_grad = attend_back(
        low, blended_grad, log_totals, cos_table, sine_table, segment_ids
    )
    projected_grad, gate_up_part, down_part, output_part = lax.optimization_barrier(
        (projected_grad, gate_up_part, down_part, output_part)
    )
    gate_up_sum = total(gate_up_part)
    down_sum = total(down_part)
    output_sum = total(output_part)
    first_block = dot(normed_one, projected_grad, ((0,), (1,))).astype(jnp.bfloat16)
    first_part = scatter(
        jnp.concatenate(
            [
                into_grid(first_block[:, :query_width], row_count, col_count),
                into_grid(
                    first_block[:, query_width : query_width + kv_width], row_count, col_count
                ),
                into_grid(first_block[:, query_width + kv_width :], row_count, col_count),
            ],
            axis=2,
        )
    )
    first_part, gate_up_sum, down_sum, output_sum = lax.optimization_barrier(
        (first_part, gate_up_sum, down_sum, output_sum)
    )
    first_sum = total(first_part)
    normed_one_grad = dot(projected_grad, first_low, ((0,), (1,)))
    gain_one, input_part = norm_backward(inputs, inverse_one, norm_gains[0], normed_one_grad)
    input_grad = (middle_grad + input_part).astype(jnp.bfloat16)
    reduced = (
        first_sum[:, : cuts[0]],
        first_sum[:, cuts[0] : cuts[1]],
        first_sum[:, cuts[1] :],
        output_sum,
        gate_up_sum,
        down_sum,
    )
    gains_grad = lax.psum(jnp.stack([gain_one, gain_two]), ("dp", "row", "col"))
    query_update = adam_step(
        query_weight, reduced[0], query_moment, query_square, matrix_rate, decay_rate
    )
    key_update = adam_step(key_weight, reduced[1], key_moment, key_square, matrix_rate, decay_rate)
    value_update = adam_step(
        value_weight, reduced[2], value_moment, value_square, matrix_rate, decay_rate
    )
    output_update = adam_step(
        output_weight, reduced[3], output_moment, output_square, matrix_rate, decay_rate
    )
    gate_up_update = adam_step(
        gate_up_weight, reduced[4], gate_up_moment, gate_up_square, matrix_rate, decay_rate
    )
    down_update = adam_step(
        down_weight, reduced[5], down_moment, down_square, matrix_rate, decay_rate
    )
    gains_update = adam_step(norm_gains, gains_grad, gains_moment, gains_square, gain_rate, 0.0)
    return (
        block_out,
        input_grad,
        reduced[0],
        query_update[0],
        query_update[1],
        query_update[2],
        reduced[1],
        key_update[0],
        key_update[1],
        key_update[2],
        reduced[2],
        value_update[0],
        value_update[1],
        value_update[2],
        reduced[3],
        output_update[0],
        output_update[1],
        output_update[2],
        reduced[4],
        gate_up_update[0],
        gate_up_update[1],
        gate_up_update[2],
        reduced[5],
        down_update[0],
        down_update[1],
        down_update[2],
        gains_grad,
        gains_update[0],
        gains_update[1],
        gains_update[2],
    )


def solution(mesh):
    in_specs = (
        P(("dp", "row", "col"), None),
        P(("dp", "row", "col"), None),
        P(("dp", "row", "col")),
        P(("dp", "row", "col")),
        P("row", "col"),
        P("row", "col"),
        P("row", "col"),
        P("row", "col"),
        P(None, "row", "col"),
        P("row", "col"),
        P(),
        P("row", "col"),
        P("row", "col"),
        P("row", "col"),
        P("row", "col"),
        P(None, "row", "col"),
        P("row", "col"),
        P(),
        P("row", "col"),
        P("row", "col"),
        P("row", "col"),
        P("row", "col"),
        P(None, "row", "col"),
        P("row", "col"),
        P(),
    )
    out_specs = (
        P(("dp", "row", "col"), None),
        P(("dp", "row", "col"), None),
        P("row", "col"),
        P("row", "col"),
        P("row", "col"),
        P("row", "col"),
        P("row", "col"),
        P("row", "col"),
        P("row", "col"),
        P("row", "col"),
        P("row", "col"),
        P("row", "col"),
        P("row", "col"),
        P("row", "col"),
        P("row", "col"),
        P("row", "col"),
        P("row", "col"),
        P("row", "col"),
        P(None, "row", "col"),
        P(None, "row", "col"),
        P(None, "row", "col"),
        P(None, "row", "col"),
        P("row", "col"),
        P("row", "col"),
        P("row", "col"),
        P("row", "col"),
        P(),
        P(),
        P(),
        P(),
    )
    return jax.shard_map(shards, mesh=mesh, in_specs=in_specs, out_specs=out_specs, check_vma=False)
```

time: 1030 us -> 650 us (0.63)
  matrix products: 272 us -> 32.6 us
  Pallas kernels: 0 us -> 148 us
  waiting for transfers between devices: 357 us -> 248 us
  other arithmetic: 147 us -> 51 us
  local copies, waits for them, and re-layouts: 157 us -> 103 us
  blocking collectives: 65.1 us -> 41.7 us
    dot_general x53 -> x6, matrix products: 272 us -> 32.6 us  [dot(): lax.dot_general(left, right, (dims, ((), ())), preferred_element_type=jnp...]
    pallas_call x0 -> x3, Pallas kernels: none -> 148 us  [the longest x1 74.6 us: mlp(): pl.pallas_call(mlp_kernel, grid=(cols,), in_specs=[fixed(token_count, fea...]
    reduce_scatter x6 -> x4, waiting for transfers between devices: 250 us -> 175 us  [scatter(): lax.psum_scatter(stack, ('row', 'col'), scatter_dimension=0, tiled=True)[0]]
    psum x1 -> x2, waiting for transfers between devices: 86.3 us -> 29.8 us  [total(): return lax.psum(part, 'dp').astype(jnp.float32)]
    convert_element_type x20 -> x6, other arithmetic: 57 us -> 8.56 us  [the longest x3 5.22 us: total(): return lax.psum(part, 'dp').astype(jnp.float32)]
    dot_general x8 -> x0, local copies, waits for them, and re-layouts: 31.8 us -> none  [the longest x5 10 us: project_back(): jnp.einsum('tcb,rcab->tra', shaped, grid, preferred_element_type=jnp.floa...]
    slice x1 -> x0, other arithmetic: 30.1 us -> none  [shards(): gate_pre = paired[0]]
    transpose x6 -> x4, local copies, waits for them, and re-layouts: 32.3 us -> 6.95 us  [into_grid(): whole.reshape(row_count, height, col_count, width).transpose(0, 2, 1, 3)]
  transfers between devices with their start and end apart: 11 -> 9, of which waited for: 5 -> 7; matrix products, arithmetic and copies ran while one was open for 24% -> 21% of each run, Pallas kernels for 0% -> 11%
where the time goes in v1:
time: 650 us; the launch traced here: 640 us
  waiting for transfers between devices  248 us (38%)
  Pallas kernels  148 us (23%)
  local copies, waits for them, and re-layouts  103 us (16%)
  other arithmetic  51 us (8%)
  blocking collectives  41.7 us (6%)
  matrix products  32.6 us (5%)
  between operations  15 us (2%)
    reduce_scatter x4, waiting for transfers between devices, scatter(): lax.psum_scatter(stack, ('row', 'col'), scatter_dimension=0, tiled=True)[0]  175 us
    pallas_call x1, Pallas kernels, mlp(): pl.pallas_call(mlp_kernel, grid=(cols,), in_specs=[fixed(token_count, fea...  74.6 us
    all_gather x3, waiting for transfers between devices, gather(): return lax.all_gather(block[None], ('row', 'col'), axis=0, tiled=True)  42.4 us
    pallas_call x1, Pallas kernels, attend_back(): pl.pallas_call(attend_back_kernel, grid=(KV_HEADS,), in_specs=head_specs(...  42 us
    psum x1, blocking collectives, shards(): gains_grad = lax.psum(jnp.stack([gain_one, gain_two]), ('dp', 'row', 'col'))  41.7 us
    dot_general x6, matrix products, dot(): lax.dot_general(left, right, (dims, ((), ())), preferred_element_type=jnp...  32.6 us
    pallas_call x1, Pallas kernels, attend(): pl.pallas_call(attend_kernel, grid=(KV_HEADS,), in_specs=head_specs() + [...  31.2 us
    psum x2, waiting for transfers between devices, total(): return lax.psum(part, 'dp').astype(jnp.float32)  29.8 us
  transfers between devices with their start and end apart: 9, of which 7 were waited for; matrix products, arithmetic and copies ran while one was open for 21% of the time, Pallas kernels for 11%

profile of v1, /device:TPU:0, one launch (start us, length us, event | category | flops | bytes accessed | tf_op | source)
XLA Modules:
  0.0 639.8 jit_solution(12195677503198027537)
XLA Ops:
  11.8 2.2 convert_element_type.64
  15.6 4.1 copy.128.back_ref
  21.3 33.0 %all-gather.6.cloned.1.call-done = bf16[8,480,640]{2,1,0:T(8,128)(2,1)} async-done(((bf16[1,480,640]{2,1,0:T(8,128)(2,1)}), bf16[8,480,640]{2,1,0:T(8,128)(2,1)}) %all-gather.6.cloned.1.call-update) | async-done | bytes 4915216 | tf_op jit(solution)/shard_map/all_gather | solution.py:439
  54.4 4.5 fusion.29
  58.9 2.8 copy.145
  61.6 4.9 reshape.238
  66.5 4.3 copy.146
  70.9 4.8 reshape.230
  75.7 4.1 fusion.30
  79.8 2.6 copy.122
  83.8 2.4 copy.121
  89.2 2.2 copy.124
  91.5 6.0 concatenate.30
  97.4 7.8 %fusion.15.q_ref.k_ref.v_ref = f32[1600,1024]{1,0:T(8,128)} fusion(bf16[960,1600]{1,0:T(8,128)(2,1)} %concatenate.30, bf16[1024,960]{0,1:T(8,128)(2,1)S(1)} %copy-done.11, f32[960]{0:T(1024)S(1)} %bitcast.95, f32[1024]{0:T(1024)S(1)} %get-tuple-element.227), kind=kOutput, calls=%fused_computation.41 | convolution fusion | flops 3149660160 | bytes 11599616 | tf_op jit(solution)/shard_map/dot_general | solution.py:47
  105.3 31.2 %attend.1 = (bf16[1600,1024]{1,0:T(8,128)(2,1)S(1)}, bf16[960,1024]{1,0:T(8,128)(2,1)S(1)}, f32[5,3,1024]{2,1,0:T(4,128)S(1)}) custom-call(f32[1600,1024]{1,0:T(8,128)} %fusion.15.q_ref.k_ref.v_ref, f32[1600,1024]{1,0:T(8,128)} %fusion.15.q_ref.k_ref.v_ref, f32[1600,1024]{1,0:T(8,128)} %fusion.15.q_ref.k_ref.v_ref, ...), custom_call_target="tpu_custom_call" | custom-call | flops 20132659200 | bytes 16777216 | tf_op jit(solution)/shard_map/attend/pallas_call | solution.py:166
  136.5 2.6 multiply_reduce_fusion.2
  139.1 1.9 copy-done.4
  142.6 3.9 copy.127.normed_ref
  146.5 3.8 fusion.41.normed_turned
  150.3 9.3 %all-gather.8.cloned.1.call-done = bf16[16,480,640]{2,1,0:T(8,128)(2,1)} async-done(((bf16[2,480,640]{2,1,0:T(8,128)(2,1)}), bf16[16,480,640]{2,1,0:T(8,128)(2,1)}) %all-gather.8.cloned.1.call-update) | async-done | bytes 9830416 | tf_op jit(solution)/shard_map/all_gather | solution.py:439
  159.6 74.6 %mlp.1 = (f32[1024,960]{1,0:T(8,128)}, f32[1024,960]{1,0:T(8,128)}, bf16[2,4,2,480,640]{4,3,2,1,0:T(8,128)(2,1)}, bf16[2,4,480,640]{3,2,1,0:T(8,128)(2,1)}) custom-call(bf16[1024,960]{1,0:T(8,128)(2,1)} %copy.127.normed_ref, bf16[960,1024]{1,0:T(8,128)(2,1)} %fusion.41.normed_turned, bf16[1024,960]{1,0:T(8,128)(2,1)} %copy.128.back_ref, ...), custom_call_target="tpu_custom_call" | custom-call | flops 45298483200 | bytes 67108864 | tf_op jit(solution)/shard_map/mlp/pallas_call | solution.py:327
  234.2 5.4 copy.129
  239.6 5.3 copy.130
  244.9 4.5 multiply_reduce_fusion
  250.5 5.3 subtract_add_fusion
  255.9 2.0 copy-done.7
  257.8 3.5 convolution_convert_fusion.1
  261.4 5.3 reshape.243
  270.4 4.3 convolution_convert_fusion.2.grad_ref
  274.8 42.0 %attend_back.1 = bf16[1600,1024]{1,0:T(8,128)(2,1)S(1)} custom-call(bf16[1600,1024]{1,0:T(8,128)(2,1)} %copy-done.3, bf16[1600,1024]{1,0:T(8,128)(2,1)} %copy-done.3, bf16[1600,1024]{1,0:T(8,128)(2,1)} %copy-done.3, bf16[960,1024]{1,0:T(8,128)(2,1)S(1)} %convolution_convert_fusion.2.grad_ref, f32[5,3,1024]{2,1,0:T(4,128)S(1)} %get-tuple-element.49.log_ref, ...), custom_call_target="tpu_custom_call" | custom-call | flops 60397977600 | bytes 16777216 | tf_op jit(solution)/shard_map/attend_back/pallas_call | solution.py:208
  318.5 48.9 %reduce-scatter.7.cloned.1.call-done = bf16[1,480,640]{2,1,0:T(8,128)(2,1)} async-done(((bf16[8,480,640]{2,1,0:T(8,128)(2,1)}), bf16[1,480,640]{2,1,0:T(8,128)(2,1)}) %reduce-scatter.7.cloned.1.call-update) | async-done | bytes 614416 | tf_op jit(solution)/shard_map/reduce_scatter | solution.py:442
  367.4 81.7 %reduce-scatter.5.cloned.1.call-done = bf16[1,2,480,640]{3,2,1,0:T(8,128)(2,1)} async-done(((bf16[8,2,480,640]{3,2,1,0:T(8,128)(2,1)}), bf16[1,2,480,640]{3,2,1,0:T(8,128)(2,1)}) %reduce-scatter.5.cloned.1.call-update) | async-done | bytes 1228816 | tf_op jit(solution)/shard_map/reduce_scatter | solution.py:442
  449.2 6.3 convolution_convert_fusion
  457.5 3.0 reshape.245
  460.4 3.1 copy.133
  466.5 3.5 reshape.247
  472.3 3.5 reshape.249
  476.9 1.9 pad_maximum_fusion
  480.8 8.0 %fusion.9 = (f32[960]{0:T(1024)S(1)}, f32[1024]{0:T(1024)S(1)}, f32[1024,960]{0,1:T(8,128)}) fusion(bf16[1024,960]{0,1:T(8,128)(2,1)} %param.25, f32[1024]{0:T(1024)S(1)} %copy-done.40, f32[960]{0:T(1024)S(1)} %bitcast.97, bf16[960,1600]{1,0:T(8,128)(2,1)} %concatenate.30, bf16[1600,1024]{1,0:T(8,128)(2,1)S(1)} %copy-done.2), kind=kOutput, calls=%fused_computation.15 | convolution fusion | flops 3152607232 | bytes 12262912 | tf_op jit(solution)/shard_map/dot_general | solution.py:47
  488.8 41.7 %psum.39 = f32[2,960]{1,0:T(2,128)S(1)} all-reduce(f32[2,960]{1,0:T(2,128)S(1)} %pad_maximum_fusion.2), channel_id=1, replica_groups=mesh['dp'=4,'row'=2,'col'=4] {'dp','row','col'}, use_global_device_ids=true, to_apply=%region_14.0 | all-reduce | flops 1920 | bytes 15360 | tf_op jit(solution)/shard_map/psum | solution.py:524
  531.2 6.1 fusion.6
  537.3 2.6 all-reduce.6.cloned.1.call-done
  541.0 3.1 convert_element_type.72
  545.2 44.4 %reduce-scatter.11.cloned.1.call-done = bf16[1,480,400]{1,2,0:T(8,128)(2,1)} async-done(((bf16[8,480,400]{1,2,0:T(8,128)(2,1)}), bf16[1,480,400]{1,2,0:T(8,128)(2,1)}) %reduce-scatter.11.cloned.1.call-update) | async-done | bytes 384016 | tf_op jit(solution)/shard_map/reduce_scatter | solution.py:442
  589.7 2.7 multiply_subtract_fusion.2
  592.4 6.9 %multiply_subtract_fusion = (f32[2,480,640]{2,1,0:T(8,128)}, f32[2,480,640]{2,1,0:T(8,128)}, f32[2,480,640]{2,1,0:T(8,128)}) fusion(f32[2,480,640]{2,1,0:T(8,128)S(1)} %copy-done.9, f32[2,480,640]{2,1,0:T(8,128)S(1)} %copy-done.10, f32[2,480,640]{2,1,0:T(8,128)} %param.47, f32[2,480,640]{2,1,0:T(8,128)} %param.40), kind=kLoop, calls=%fused_computation.26 | loop fusion | flops 9216000 | bytes 17203200 | tf_op jit(solution)/shard_map/sub | solution.py:400
  599.4 2.4 multiply_subtract_fusion.1
  601.8 27.2 %all-reduce.4.cloned.1.call-done = bf16[480,400]{0,1:T(8,128)(2,1)} async-done(((bf16[480,400]{0,1:T(8,128)(2,1)}), bf16[480,400]{0,1:T(8,128)(2,1)}) %all-reduce.4.cloned.1.call-update) | async-done | bytes 384016 | tf_op jit(solution)/shard_map/psum | solution.py:445
  (144 shorter events, 37.2 us)
Async XLA Ops:
  7.2 47.2 %all-gather.6.cloned.1.call-start = ((), (), s32[]{:S(2)}) async-start(), calls=%async_computation.4 | async-start | bytes 5529600 | tf_op jit(solution)/shard_map/all_gather | solution.py:439
  10.6 3.5 copy-start.8
  11.8 138.5 %all-gather.10.cloned.1.call-start = ((), (), s32[]{:S(2)}) async-start(), calls=%async_computation.11 | async-start | bytes 5529600 | tf_op jit(solution)/shard_map/all_gather | solution.py:439
  14.1 145.5 %all-gather.8.cloned.1.call-start = ((), (), s32[]{:S(2)}) async-start(), calls=%async_computation.10 | async-start | bytes 11059200 | tf_op jit(solution)/shard_map/all_gather | solution.py:439
  15.3 4.4 copy-start.11
  15.3 303.1 %reduce-scatter.9.cloned.1.call-start = ((), (), s32[]{:S(2)}) async-start(), calls=%async_computation.7 | async-start | bytes 2211840 | tf_op jit(solution)/shard_map/reduce_scatter | solution.py:442
  15.6 5.1 copy-start.35
  20.8 76.7 %copy-start.39 = (f32[1024]{0:T(1024)}, f32[1024]{0:T(1024)S(1)}, u32[]{:S(2)}) copy-start(f32[1024]{0:T(1024)S(1)} %get-tuple-element.227) | copy-start | bytes 12292
  20.8 76.7 %copy-start.41 = (f32[1,960]{1,0:T(1,128)}, f32[1,960]{1,0:T(1,128)S(1)}, u32[]{:S(2)}) copy-start(f32[1,960]{1,0:T(1,128)S(1)} %get-tuple-element.223) | copy-start | bytes 11524
  105.3 31.2 %copy-start.12 = (bf16[1024,960]{0,1:T(8,128)(2,1)S(1)}, bf16[1024,960]{0,1:T(8,128)(2,1)}, u32[]{:S(2)}) copy-start(bf16[1024,960]{0,1:T(8,128)(2,1)} %param.25) | copy-start | bytes 5898244
  105.3 31.2 %copy-start.17 = (bf16[960,960]{1,0:T(8,128)(2,1)S(1)}, bf16[960,960]{1,0:T(8,128)(2,1)}, u32[]{:S(2)}) copy-start(bf16[960,960]{1,0:T(8,128)(2,1)} %reshape.238) | copy-start | bytes 5529604
  136.4 2.6 copy-start.3
  139.0 1.9 copy-start.4
  244.9 4.5 copy-start.5
  244.9 5.6 copy-start.6
  255.9 2.0 copy-start.7
  268.2 99.1 %reduce-scatter.7.cloned.1.call-start = ((), (), s32[]{:S(2)}) async-start(), calls=%async_computation.6 | async-start | bytes 5529600 | tf_op jit(solution)/shard_map/reduce_scatter | solution.py:442
  268.8 180.3 %reduce-scatter.5.cloned.1.call-start = ((), (), s32[]{:S(2)}) async-start(), calls=%async_computation.5 | async-start | bytes 11059200 | tf_op jit(solution)/shard_map/reduce_scatter | solution.py:442
  269.4 270.5 %all-reduce.6.cloned.1.call-start = ((), (), s32[]{:S(2)}) async-start(), calls=%async_computation.12 | async-start | bytes 4177920 | tf_op jit(solution)/shard_map/psum | solution.py:445
  274.7 174.4 %copy-start.13 = (bf16[1024,960]{0,1:T(8,128)(2,1)S(1)}, bf16[1024,960]{0,1:T(8,128)(2,1)}, u32[]{:S(2)}) copy-start(bf16[1024,960]{0,1:T(8,128)(2,1)} %param.25) | copy-start | bytes 5898244
  274.8 174.4 %copy-start.40 = (f32[1024]{0:T(1024)S(1)}, f32[1024]{0:T(1024)}, u32[]{:S(2)}) copy-start(f32[1024]{0:T(1024)} %copy-done.39) | copy-start | bytes 12292
  274.8 174.4 %copy-start.42 = (f32[1,960]{1,0:T(1,128)S(1)}, f32[1,960]{1,0:T(1,128)}, u32[]{:S(2)}) copy-start(f32[1,960]{1,0:T(1,128)} %copy-done.41) | copy-start | bytes 11524
  449.1 140.5 %reduce-scatter.11.cloned.1.call-start = ((), (), s32[]{:S(2)}) async-start(), calls=%async_computation.8 | async-start | bytes 3686400 | tf_op jit(solution)/shard_map/reduce_scatter | solution.py:442
  478.9 1.9 copy-start.2
  478.9 51.7 %copy-start.36 = (f32[2,960]{1,0:T(2,128)S(1)}, f32[2,960]{1,0:T(2,128)}, u32[]{:S(2)}) copy-start(f32[2,960]{1,0:T(2,128)} %param.35) | copy-start | bytes 23044
  478.9 51.6 %copy-start.43 = (f32[2,960]{1,0:T(2,128)S(1)}, f32[2,960]{1,0:T(2,128)}, u32[]{:S(2)}) copy-start(f32[2,960]{1,0:T(2,128)} %param.49) | copy-start | bytes 23044
  478.9 51.6 %copy-start.44 = (f32[2,960]{1,0:T(2,128)S(1)}, f32[2,960]{1,0:T(2,128)}, u32[]{:S(2)}) copy-start(f32[2,960]{1,0:T(2,128)} %param.42) | copy-start | bytes 23044
  478.9 52.3 %copy-start.38 = (f32[1024]{0:T(1024)S(1)}, f32[1024]{0:T(1024)}, u32[]{:S(2)}) copy-start(f32[1024]{0:T(1024)} %get-tuple-element.226) | copy-start | bytes 12292
  478.9 150.0 %all-reduce.4.cloned.1.call-start = ((), (), s32[]{:S(2)}) async-start(), calls=%async_computation.9 | async-start | bytes 819200 | tf_op jit(solution)/shard_map/psum | solution.py:445
  530.5 6.8 %copy-start.37 = (f32[2,960]{1,0:T(2,128)}, f32[2,960]{1,0:T(2,128)S(1)}, u32[]{:S(2)}) copy-start(f32[2,960]{1,0:T(2,128)S(1)} %psum.39) | copy-start | bytes 23044
  539.9 4.1 copy-start.28
  541.0 48.7 %copy-start.21 = (f32[480,240]{1,0:T(8,128)}, f32[480,240]{1,0:T(8,128)S(1)}, u32[]{:S(2)}) copy-start(f32[480,240]{1,0:T(8,128)S(1)} %convert_element_type.74) | copy-start | bytes 1382404
  541.0 48.7 %copy-start.19 = (f32[480,240]{1,0:T(8,128)S(1)}, f32[480,240]{1,0:T(8,128)}, u32[]{:S(2)}) copy-start(f32[480,240]{1,0:T(8,128)} %param.32) | copy-start | bytes 1382404
  544.1 48.3 %copy-start.9 = (f32[2,480,640]{2,1,0:T(8,128)S(1)}, f32[2,480,640]{2,1,0:T(8,128)}, u32[]{:S(2)}) copy-start(f32[2,480,640]{2,1,0:T(8,128)} %param.33) | copy-start | bytes 7372804
  589.6 2.7 copy-start.10
  592.3 7.0 %copy-start.14 = (f32[480,640]{1,0:T(8,128)S(1)}, f32[480,640]{1,0:T(8,128)}, u32[]{:S(2)}) copy-start(f32[480,640]{1,0:T(8,128)} %param.34) | copy-start | bytes 3686404
  592.4 7.0 %copy-start.15 = (f32[480,640]{1,0:T(8,128)S(1)}, f32[480,640]{1,0:T(8,128)}, u32[]{:S(2)}) copy-start(f32[480,640]{1,0:T(8,128)} %convert_element_type.73) | copy-start | bytes 3686404
  592.4 7.0 %copy-start.24 = (f32[480,640]{1,0:T(8,128)S(1)}, f32[480,640]{1,0:T(8,128)}, u32[]{:S(2)}) copy-start(f32[480,640]{1,0:T(8,128)} %param.48) | copy-start | bytes 3686404
  592.4 7.0 %copy-start.25 = (f32[480,640]{1,0:T(8,128)S(1)}, f32[480,640]{1,0:T(8,128)}, u32[]{:S(2)}) copy-start(f32[480,640]{1,0:T(8,128)} %param.41) | copy-start | bytes 3686404
  599.3 30.9 %copy-start.20 = (f32[480,240]{1,0:T(8,128)S(1)}, f32[480,240]{1,0:T(8,128)}, u32[]{:S(2)}) copy-start(f32[480,240]{1,0:T(8,128)} %param.29) | copy-start | bytes 1382404
  599.4 30.9 %copy-start.29 = (f32[480,240]{1,0:T(8,128)S(1)}, f32[480,240]{1,0:T(8,128)}, u32[]{:S(2)}) copy-start(f32[480,240]{1,0:T(8,128)} %param.43) | copy-start | bytes 1382404
  599.4 30.9 %copy-start.30 = (f32[480,240]{1,0:T(8,128)S(1)}, f32[480,240]{1,0:T(8,128)}, u32[]{:S(2)}) copy-start(f32[480,240]{1,0:T(8,128)} %param.36) | copy-start | bytes 1382404
  601.8 29.9 %copy-start.26 = (f32[480,80]{0,1:T(8,128)S(1)}, f32[480,80]{0,1:T(8,128)}, u32[]{:S(2)}) copy-start(f32[480,80]{0,1:T(8,128)} %param.31) | copy-start | bytes 460804
  601.8 29.9 %copy-start.27 = (f32[480,80]{0,1:T(8,128)S(1)}, f32[480,80]{0,1:T(8,128)}, u32[]{:S(2)}) copy-start(f32[480,80]{0,1:T(8,128)} %param.30) | copy-start | bytes 460804
  601.8 29.9 %copy-start.31 = (f32[480,80]{0,1:T(8,128)S(1)}, f32[480,80]{0,1:T(8,128)}, u32[]{:S(2)}) copy-start(f32[480,80]{0,1:T(8,128)} %param.45) | copy-start | bytes 460804
  601.8 29.9 %copy-start.32 = (f32[480,80]{0,1:T(8,128)S(1)}, f32[480,80]{0,1:T(8,128)}, u32[]{:S(2)}) copy-start(f32[480,80]{0,1:T(8,128)} %param.38) | copy-start | bytes 460804
  629.0 2.7 copy-start.23
  630.3 2.6 copy-start.22
  (7 other events, 10.3 us)
Sparse Core Ops, SparseCore 0:
  11.9 42.4 all-gather.5
  56.8 39.7 all-gather.9
  99.1 60.4 all-gather.7
  268.3 40.3 reduce-scatter.8
  312.5 54.8 reduce-scatter.6
  370.8 78.2 reduce-scatter.4
  451.7 88.2 all-reduce.5
  543.7 45.8 reduce-scatter.10
  592.1 36.8 all-reduce.3

commit v2 on v1

--- a/solution.py
+++ b/solution.py
@@ -482,17 +482,15 @@
     middle_grad = cotangent.astype(jnp.float32) + middle_part
     middle_low = middle_grad.astype(jnp.bfloat16)
     output_block = dot(blended, middle_low, ((1,), (0,))).astype(jnp.bfloat16)
-    output_part = scatter(into_grid(output_block, row_count, col_count))
     blended_grad = dot(output_low, middle_low, ((1,), (1,))).astype(jnp.bfloat16)
     projected_grad = attend_back(
         low, blended_grad, log_totals, cos_table, sine_table, segment_ids
     )
-    projected_grad, gate_up_part, down_part, output_part = lax.optimization_barrier(
-        (projected_grad, gate_up_part, down_part, output_part)
+    projected_grad, gate_up_part, down_part = lax.optimization_barrier(
+        (projected_grad, gate_up_part, down_part)
     )
     gate_up_sum = total(gate_up_part)
     down_sum = total(down_part)
-    output_sum = total(output_part)
     first_block = dot(normed_one, projected_grad, ((0,), (1,))).astype(jnp.bfloat16)
     first_part = scatter(
         jnp.concatenate(
@@ -502,12 +500,13 @@
                     first_block[:, query_width : query_width + kv_width], row_count, col_count
                 ),
                 into_grid(first_block[:, query_width + kv_width :], row_count, col_count),
+                into_grid(output_block, row_count, col_count),
             ],
             axis=2,
         )
     )
-    first_part, gate_up_sum, down_sum, output_sum = lax.optimization_barrier(
-        (first_part, gate_up_sum, down_sum, output_sum)
+    first_part, gate_up_sum, down_sum = lax.optimization_barrier(
+        (first_part, gate_up_sum, down_sum)
     )
     first_sum = total(first_part)
     normed_one_grad = dot(projected_grad, first_low, ((0,), (1,)))
@@ -516,8 +515,8 @@
     reduced = (
         first_sum[:, : cuts[0]],
         first_sum[:, cuts[0] : cuts[1]],
-        first_sum[:, cuts[1] :],
-        output_sum,
+        first_sum[:, cuts[1] : cuts[2]],
+        first_sum[:, cuts[2] :],
         gate_up_sum,
         down_sum,
     )

time: 650 us -> 589 us (0.906)
  waiting for transfers between devices: 248 us -> 150 us
  local copies, waits for them, and re-layouts: 103 us -> 137 us
    reduce_scatter x4 -> x3, waiting for transfers between devices: 175 us -> 77.1 us  [scatter(): lax.psum_scatter(stack, ('row', 'col'), scatter_dimension=0, tiled=True)[0]]
    unnamed x96 -> x107, local copies, waits for them, and re-layouts: 17.7 us -> 36.2 us
    reshape x4 -> x6, local copies, waits for them, and re-layouts: 15.3 us -> 27.8 us  [into_grid(): whole.reshape(row_count, height, col_count, width).transpose(0, 2, 1, 3)]
    sub x6 -> x5, other arithmetic: 15.1 us -> 13.7 us  [adam_step(): weight - step_rate * (scaled_step + decay_factor * weight)]
  transfers between devices with their start and end apart: 9 -> 8, of which waited for: 7 -> 5; matrix products, arithmetic and copies ran while one was open for 21% -> 34% of each run, Pallas kernels for 11% -> 13%
where the time goes in v2:
time: 589 us; the launch traced here: 578 us
  waiting for transfers between devices  150 us (25%)
  Pallas kernels  147 us (25%)
  local copies, waits for them, and re-layouts  137 us (23%)
  other arithmetic  53.7 us (9%)
  blocking collectives  39.7 us (7%)
  matrix products  34.7 us (6%)
  between operations  15.1 us (3%)
    reduce_scatter x3, waiting for transfers between devices, scatter(): lax.psum_scatter(stack, ('row', 'col'), scatter_dimension=0, tiled=True)[0]  77.1 us
    pallas_call x1, Pallas kernels, mlp(): pl.pallas_call(mlp_kernel, grid=(cols,), in_specs=[fixed(token_count, fea...  74.2 us
    pallas_call x1, Pallas kernels, attend_back(): pl.pallas_call(attend_back_kernel, grid=(KV_HEADS,), in_specs=head_specs(...  42 us
    psum x1, blocking collectives, shards(): gains_grad = lax.psum(jnp.stack([gain_one, gain_two]), ('dp', 'row', 'col'))  39.7 us
    all_gather x3, waiting for transfers between devices, gather(): return lax.all_gather(block[None], ('row', 'col'), axis=0, tiled=True)  39.6 us
    unnamed x107, local copies, waits for them, and re-layouts  36.2 us
    dot_general x6, matrix products, dot(): lax.dot_general(left, right, (dims, ((), ())), preferred_element_type=jnp...  34.7 us
    psum x2, waiting for transfers between devices, total(): return lax.psum(part, 'dp').astype(jnp.float32)  32.8 us
  transfers between devices with their start and end apart: 8, of which 5 were waited for; matrix products, arithmetic and copies ran while one was open for 34% of the time, Pallas kernels for 13%

profile of v2, /device:TPU:0, one launch (start us, length us, event | category | flops | bytes accessed | tf_op | source)
XLA Modules:
  0.0 578.0 jit_solution(13745233734705438326)
XLA Ops:
  11.8 2.2 convert_element_type.61
  15.6 4.1 copy.205.back_ref
  21.3 33.0 %all-gather.6.cloned.1.call-done = bf16[8,480,640]{2,1,0:T(8,128)(2,1)} async-done(((bf16[1,480,640]{2,1,0:T(8,128)(2,1)}), bf16[8,480,640]{2,1,0:T(8,128)(2,1)}) %all-gather.6.cloned.1.call-update) | async-done | bytes 4915216 | tf_op jit(solution)/shard_map/all_gather | solution.py:439
  54.4 4.4 fusion.29
  58.8 2.8 copy.235
  61.6 4.9 reshape.230
  66.5 4.1 fusion.30
  70.6 2.4 copy.198
  76.0 3.6 copy.199
  79.5 3.4 reshape.234
  82.9 2.2 copy.201
  85.1 4.4 copy.234
  89.5 4.9 reshape.238
  94.4 6.0 %concatenate.30 = bf16[960,1600]{1,0:T(8,128)(2,1)} concatenate(bf16[960,960]{1,0:T(8,128)(2,1)} %reshape.230, bf16[960,320]{1,0:T(8,128)(2,1)S(1)} %copy.200, bf16[960,320]{1,0:T(8,128)(2,1)} %copy.201), dimensions={1} | concatenate | bytes 6144000 | tf_op jit(solution)/shard_map/concatenate | solution.py:454
  100.4 7.8 %fusion.15.q_ref.k_ref.v_ref = f32[1600,1024]{1,0:T(8,128)} fusion(bf16[960,1600]{1,0:T(8,128)(2,1)} %concatenate.30, bf16[1024,960]{0,1:T(8,128)(2,1)S(1)} %copy-done.10, f32[960]{0:T(1024)S(1)} %bitcast.93, f32[1024]{0:T(1024)S(1)} %get-tuple-element.257), kind=kOutput, calls=%fused_computation.41 | convolution fusion | flops 3149660160 | bytes 11599616 | tf_op jit(solution)/shard_map/dot_general | solution.py:47
  108.2 31.1 %attend.1 = (bf16[1600,1024]{1,0:T(8,128)(2,1)S(1)}, bf16[960,1024]{1,0:T(8,128)(2,1)S(1)}, f32[5,3,1024]{2,1,0:T(4,128)S(1)}) custom-call(f32[1600,1024]{1,0:T(8,128)} %fusion.15.q_ref.k_ref.v_ref, f32[1600,1024]{1,0:T(8,128)} %fusion.15.q_ref.k_ref.v_ref, f32[1600,1024]{1,0:T(8,128)} %fusion.15.q_ref.k_ref.v_ref, ...), custom_call_target="tpu_custom_call" | custom-call | flops 20132659200 | bytes 16777216 | tf_op jit(solution)/shard_map/attend/pallas_call | solution.py:166
  139.3 2.5 multiply_reduce_fusion.2
  145.4 3.9 copy.204.normed_ref
  149.3 3.8 fusion.42.normed_turned
  153.1 6.5 %all-gather.8.cloned.1.call-done = bf16[16,480,640]{2,1,0:T(8,128)(2,1)} async-done(((bf16[2,480,640]{2,1,0:T(8,128)(2,1)}), bf16[16,480,640]{2,1,0:T(8,128)(2,1)}) %all-gather.8.cloned.1.call-update) | async-done | bytes 9830416 | tf_op jit(solution)/shard_map/all_gather | solution.py:439
  159.6 74.2 %mlp.1 = (f32[1024,960]{1,0:T(8,128)}, f32[1024,960]{1,0:T(8,128)}, bf16[2,4,2,480,640]{4,3,2,1,0:T(8,128)(2,1)}, bf16[2,4,480,640]{3,2,1,0:T(8,128)(2,1)}) custom-call(bf16[1024,960]{1,0:T(8,128)(2,1)} %copy.204.normed_ref, bf16[960,1024]{1,0:T(8,128)(2,1)} %fusion.42.normed_turned, bf16[1024,960]{1,0:T(8,128)(2,1)} %copy.205.back_ref, ...), custom_call_target="tpu_custom_call" | custom-call | flops 45298483200 | bytes 67108864 | tf_op jit(solution)/shard_map/mlp/pallas_call | solution.py:327
  234.4 5.4 copy.207
  239.8 5.6 copy.206
  245.4 5.0 multiply_reduce_fusion
  251.6 5.3 subtract_add_fusion
  256.9 5.2 convolution_convert_fusion.2.grad_ref
  262.1 42.0 %attend_back.1 = bf16[1600,1024]{1,0:T(8,128)(2,1)S(1)} custom-call(bf16[1600,1024]{1,0:T(8,128)(2,1)} %copy-done.3, bf16[1600,1024]{1,0:T(8,128)(2,1)} %copy-done.3, bf16[1600,1024]{1,0:T(8,128)(2,1)} %copy-done.3, bf16[960,1024]{1,0:T(8,128)(2,1)S(1)} %convolution_convert_fusion.2.grad_ref, f32[5,3,1024]{2,1,0:T(4,128)S(1)} %get-tuple-element.47.log_ref, ...), custom_call_target="tpu_custom_call" | custom-call | flops 60397977600 | bytes 16777216 | tf_op jit(solution)/shard_map/attend_back/pallas_call | solution.py:208
  306.1 64.9 %reduce-scatter.4.cloned.1.call-done = bf16[1,2,480,640]{3,2,1,0:T(8,128)(2,1)} async-done(((bf16[8,2,480,640]{3,2,1,0:T(8,128)(2,1)}), bf16[1,2,480,640]{3,2,1,0:T(8,128)(2,1)}) %reduce-scatter.4.cloned.1.call-update) | async-done | bytes 1228816 | tf_op jit(solution)/shard_map/reduce_scatter | solution.py:442
  371.0 5.6 convolution_convert_fusion.1
  376.7 6.2 %reshape.249 = bf16[2,480,4,240]{3,2,1,0:T(4,128)(2,1)} reshape(bf16[960,960]{1,0:T(8,128)(2,1)} %convolution_convert_fusion.1) | data formatting | bytes 3686400 | tf_op jit(solution)/shard_map/reshape | solution.py:379
  382.9 4.4 copy.214
  387.3 5.3 convolution_convert_fusion
  395.8 6.0 %reshape.243 = bf16[2,480,4,240]{3,2,1,0:T(4,128)(2,1)} reshape(bf16[960,960]{1,0:T(8,128)(2,1)} %slice.58) | data formatting | bytes 3686400 | tf_op jit(solution)/shard_map/reshape | solution.py:379
  401.9 4.2 copy.209
  406.1 2.9 fusion.31
  408.9 2.2 copy.210
  411.1 3.5 reshape.245
  416.6 2.2 copy.212
  418.8 3.5 reshape.247
  423.5 5.3 pad_maximum_fusion
  441.0 8.2 %fusion.9 = (f32[960]{0:T(1024)S(1)}, f32[1024]{0:T(1024)S(1)}, f32[1024,960]{0,1:T(8,128)}) fusion(bf16[1024,960]{0,1:T(8,128)(2,1)} %param.25, f32[1024]{0:T(1024)S(1)} %copy-done.39, f32[960]{0:T(1024)S(1)} %bitcast.95, bf16[960,1600]{1,0:T(8,128)(2,1)} %concatenate.30, bf16[1600,1024]{1,0:T(8,128)(2,1)S(1)} %copy-done.2), kind=kOutput, calls=%fused_computation.16 | convolution fusion | flops 3152607232 | bytes 12262912 | tf_op jit(solution)/shard_map/dot_general | solution.py:47
  449.2 39.7 %psum.31 = f32[2,960]{1,0:T(2,128)S(1)} all-reduce(f32[2,960]{1,0:T(2,128)S(1)} %pad_maximum_fusion.2), channel_id=1, replica_groups=mesh['dp'=4,'row'=2,'col'=4] {'dp','row','col'}, use_global_device_ids=true, to_apply=%region_12.0 | all-reduce | flops 1920 | bytes 15360 | tf_op jit(solution)/shard_map/psum | solution.py:523
  489.6 6.2 %fusion.6 = bf16[1024,960]{0,1:T(8,128)(2,1)} fusion(f32[1024,960]{0,1:T(8,128)} %copy-done.7, bf16[1024,960]{0,1:T(8,128)(2,1)} %param.25, f32[1024,960]{0,1:T(8,128)} %get-tuple-element.262, f32[1024]{0:T(1024)S(1)} %broadcast_multiply_fusion, f32[1024]{0:T(1024)S(1)} %copy-done.37, f32[960]{0:T(1024)S(1)} %bitcast.96, f32[1024]{0:T(1024)S(1)} %copy-done.39), kind=kLoop, calls=%fused_computation.13 | loop fusion | flops 7864320 | bytes 11812608 | tf_op jit(solution)/shard_map/convert_element_type | solution.py:514
  495.8 3.1 convert_element_type.69
  500.0 12.2 %reduce-scatter.8.cloned.1.call-done = bf16[1,480,640]{1,2,0:T(8,128)(2,1)} async-done(((bf16[8,480,640]{1,2,0:T(8,128)(2,1)}), bf16[1,480,640]{1,2,0:T(8,128)(2,1)}) %reduce-scatter.8.cloned.1.call-update) | async-done | bytes 614416 | tf_op jit(solution)/shard_map/reduce_scatter | solution.py:442
  512.3 7.5 %multiply_subtract_fusion = (f32[2,480,640]{2,1,0:T(8,128)}, f32[2,480,640]{2,1,0:T(8,128)}, f32[2,480,640]{2,1,0:T(8,128)}) fusion(f32[2,480,640]{2,1,0:T(8,128)S(1)} %copy-done.9, f32[2,480,640]{2,1,0:T(8,128)} %convert_element_type.69, f32[2,480,640]{2,1,0:T(8,128)} %param.47, f32[2,480,640]{2,1,0:T(8,128)} %param.40), kind=kLoop, calls=%fused_computation.26 | loop fusion | flops 9216000 | bytes 17203200 | tf_op jit(solution)/shard_map/sub | solution.py:400
  519.9 2.4 multiply_subtract_fusion.1
  522.3 32.8 %all-reduce.4.cloned.1.call-done = bf16[480,640]{0,1:T(8,128)(2,1)} async-done(((bf16[480,640]{0,1:T(8,128)(2,1)}), bf16[480,640]{0,1:T(8,128)(2,1)}) %all-reduce.4.cloned.1.call-update) | async-done | bytes 614416 | tf_op jit(solution)/shard_map/psum | solution.py:445
  (151 shorter events, 53.9 us)
Async XLA Ops:
  7.2 47.2 %all-gather.6.cloned.1.call-start = ((), (), s32[]{:S(2)}) async-start(), calls=%async_computation.3 | async-start | bytes 5529600 | tf_op jit(solution)/shard_map/all_gather | solution.py:439
  10.6 3.5 copy-start.8
  11.8 141.3 %all-gather.10.cloned.1.call-start = ((), (), s32[]{:S(2)}) async-start(), calls=%async_computation.9 | async-start | bytes 5529600 | tf_op jit(solution)/shard_map/all_gather | solution.py:439
  14.1 145.5 %all-gather.8.cloned.1.call-start = ((), (), s32[]{:S(2)}) async-start(), calls=%async_computation.8 | async-start | bytes 11059200 | tf_op jit(solution)/shard_map/all_gather | solution.py:439
  15.3 4.4 copy-start.10
  15.3 290.7 %reduce-scatter.6.cloned.1.call-start = ((), (), s32[]{:S(2)}) async-start(), calls=%async_computation.5 | async-start | bytes 5529600 | tf_op jit(solution)/shard_map/reduce_scatter | solution.py:442
  15.6 5.1 copy-start.34
  20.8 79.6 %copy-start.38 = (f32[1024]{0:T(1024)}, f32[1024]{0:T(1024)S(1)}, u32[]{:S(2)}) copy-start(f32[1024]{0:T(1024)S(1)} %get-tuple-element.257) | copy-start | bytes 12292
  20.8 79.6 %copy-start.40 = (f32[1,960]{1,0:T(1,128)}, f32[1,960]{1,0:T(1,128)S(1)}, u32[]{:S(2)}) copy-start(f32[1,960]{1,0:T(1,128)S(1)} %get-tuple-element.253) | copy-start | bytes 11524
  108.2 31.1 %copy-start.11 = (bf16[1024,960]{0,1:T(8,128)(2,1)S(1)}, bf16[1024,960]{0,1:T(8,128)(2,1)}, u32[]{:S(2)}) copy-start(bf16[1024,960]{0,1:T(8,128)(2,1)} %param.25) | copy-start | bytes 5898244
  108.2 31.1 %copy-start.16 = (bf16[960,960]{1,0:T(8,128)(2,1)S(1)}, bf16[960,960]{1,0:T(8,128)(2,1)}, u32[]{:S(2)}) copy-start(bf16[960,960]{1,0:T(8,128)(2,1)} %reshape.238) | copy-start | bytes 5529604
  139.3 2.5 copy-start.3
  233.8 137.2 %reduce-scatter.4.cloned.1.call-start = ((), (), s32[]{:S(2)}) async-start(), calls=%async_computation.4 | async-start | bytes 11059200 | tf_op jit(solution)/shard_map/reduce_scatter | solution.py:442
  234.4 261.4 %all-reduce.6.cloned.1.call-start = ((), (), s32[]{:S(2)}) async-start(), calls=%async_computation.10 | async-start | bytes 3686400 | tf_op jit(solution)/shard_map/psum | solution.py:445
  245.4 5.1 copy-start.5
  245.4 6.2 %copy-start.6 = (f32[1024,960]{0,1:T(8,128)S(1)}, f32[1024,960]{0,1:T(8,128)}, u32[]{:S(2)}) copy-start(f32[1024,960]{0,1:T(8,128)} %copy.207) | copy-start | bytes 11796484
  256.9 5.2 copy-start.7
  371.0 141.2 %reduce-scatter.8.cloned.1.call-start = ((), (), s32[]{:S(2)}) async-start(), calls=%async_computation.6 | async-start | bytes 5898240 | tf_op jit(solution)/shard_map/reduce_scatter | solution.py:442
  382.9 4.4 copy-start.2
  382.9 4.4 copy-start.39
  382.9 4.4 copy-start.41
  428.9 126.2 %all-reduce.4.cloned.1.call-start = ((), (), s32[]{:S(2)}) async-start(), calls=%async_computation.7 | async-start | bytes 1310720 | tf_op jit(solution)/shard_map/psum | solution.py:445
  441.0 48.0 %copy-start.35 = (f32[2,960]{1,0:T(2,128)S(1)}, f32[2,960]{1,0:T(2,128)}, u32[]{:S(2)}) copy-start(f32[2,960]{1,0:T(2,128)} %param.35) | copy-start | bytes 23044
  441.0 48.0 %copy-start.42 = (f32[2,960]{1,0:T(2,128)S(1)}, f32[2,960]{1,0:T(2,128)}, u32[]{:S(2)}) copy-start(f32[2,960]{1,0:T(2,128)} %param.49) | copy-start | bytes 23044
  441.0 48.0 %copy-start.43 = (f32[2,960]{1,0:T(2,128)S(1)}, f32[2,960]{1,0:T(2,128)}, u32[]{:S(2)}) copy-start(f32[2,960]{1,0:T(2,128)} %param.42) | copy-start | bytes 23044
  441.0 48.6 %copy-start.37 = (f32[1024]{0:T(1024)S(1)}, f32[1024]{0:T(1024)}, u32[]{:S(2)}) copy-start(f32[1024]{0:T(1024)} %get-tuple-element.256) | copy-start | bytes 12292
  488.9 6.9 %copy-start.36 = (f32[2,960]{1,0:T(2,128)}, f32[2,960]{1,0:T(2,128)S(1)}, u32[]{:S(2)}) copy-start(f32[2,960]{1,0:T(2,128)S(1)} %psum.31) | copy-start | bytes 23044
  495.8 3.1 copy-start.29
  495.8 16.4 %copy-start.9 = (f32[2,480,640]{2,1,0:T(8,128)S(1)}, f32[2,480,640]{2,1,0:T(8,128)}, u32[]{:S(2)}) copy-start(f32[2,480,640]{2,1,0:T(8,128)} %param.33) | copy-start | bytes 7372804
  512.2 7.6 %copy-start.13 = (f32[480,640]{1,0:T(8,128)S(1)}, f32[480,640]{1,0:T(8,128)}, u32[]{:S(2)}) copy-start(f32[480,640]{1,0:T(8,128)} %param.34) | copy-start | bytes 3686404
  512.2 7.6 %copy-start.14 = (f32[480,640]{1,0:T(8,128)S(1)}, f32[480,640]{1,0:T(8,128)}, u32[]{:S(2)}) copy-start(f32[480,640]{1,0:T(8,128)} %convert_element_type.70) | copy-start | bytes 3686404
  512.3 7.6 %copy-start.25 = (f32[480,640]{1,0:T(8,128)S(1)}, f32[480,640]{1,0:T(8,128)}, u32[]{:S(2)}) copy-start(f32[480,640]{1,0:T(8,128)} %param.48) | copy-start | bytes 3686404
  512.3 7.5 %copy-start.26 = (f32[480,640]{1,0:T(8,128)S(1)}, f32[480,640]{1,0:T(8,128)}, u32[]{:S(2)}) copy-start(f32[480,640]{1,0:T(8,128)} %param.41) | copy-start | bytes 3686404
  519.8 36.5 %copy-start.17 = (f32[480,240]{0,1:T(8,128)S(1)}, f32[480,240]{0,1:T(8,128)}, u32[]{:S(2)}) copy-start(f32[480,240]{0,1:T(8,128)} %copy.218) | copy-start | bytes 1382404
  519.8 36.5 %copy-start.18 = (f32[480,240]{0,1:T(8,128)S(1)}, f32[480,240]{0,1:T(8,128)}, u32[]{:S(2)}) copy-start(f32[480,240]{0,1:T(8,128)} %copy.222) | copy-start | bytes 1382404
  519.9 36.5 %copy-start.19 = (f32[480,240]{0,1:T(8,128)S(1)}, f32[480,240]{0,1:T(8,128)}, u32[]{:S(2)}) copy-start(f32[480,240]{0,1:T(8,128)} %copy.215) | copy-start | bytes 1382404
  519.9 36.5 %copy-start.20 = (f32[480,240]{0,1:T(8,128)S(1)}, f32[480,240]{0,1:T(8,128)}, u32[]{:S(2)}) copy-start(f32[480,240]{0,1:T(8,128)} %copy.216) | copy-start | bytes 1382404
  519.9 36.5 %copy-start.21 = (f32[480,240]{0,1:T(8,128)S(1)}, f32[480,240]{0,1:T(8,128)}, u32[]{:S(2)}) copy-start(f32[480,240]{0,1:T(8,128)} %copy.219) | copy-start | bytes 1382404
  519.9 36.5 %copy-start.22 = (f32[480,240]{0,1:T(8,128)S(1)}, f32[480,240]{0,1:T(8,128)}, u32[]{:S(2)}) copy-start(f32[480,240]{0,1:T(8,128)} %copy.220) | copy-start | bytes 1382404
  558.4 6.2 %copy-start.24 = (f32[480,240]{0,1:T(8,128)S(1)}, f32[480,240]{0,1:T(8,128)}, u32[]{:S(2)}) copy-start(f32[480,240]{0,1:T(8,128)} %get-tuple-element.223) | copy-start | bytes 1382404
  558.4 7.1 %copy-start.23 = (f32[480,240]{0,1:T(8,128)S(1)}, f32[480,240]{0,1:T(8,128)}, u32[]{:S(2)}) copy-start(f32[480,240]{0,1:T(8,128)} %get-tuple-element.222) | copy-start | bytes 1382404
  560.5 7.0 %copy-start.12 = (bf16[480,640]{0,1:T(8,128)(2,1)S(1)}, bf16[480,640]{0,1:T(8,128)(2,1)}, u32[]{:S(2)}) copy-start(bf16[480,640]{0,1:T(8,128)(2,1)} %all-reduce.4.cloned.1.call-done) | copy-start | bytes 1843204
  566.5 3.1 copy-start.27
  566.5 3.1 copy-start.28
  566.5 3.1 copy-start.30
  566.5 3.1 copy-start.31
  566.5 3.1 copy-start.32
  566.5 3.1 copy-start.33
  (5 other events, 8.2 us)
Sparse Core Ops, SparseCore 0:
  11.9 42.4 all-gather.5
  56.8 39.7 all-gather.9
  99.1 60.4 all-gather.7
  233.9 54.8 reduce-scatter.5
  292.6 78.2 reduce-scatter.3
  373.4 78.7 all-reduce.5
  456.0 56.1 reduce-scatter.7
  514.6 40.4 all-reduce.3
